TPU v7x, 256 devices: a whole 4x4x8 slice. The times are simulated.
256 devices in a mesh: seq: 128 (over y, z, x), head: 2 (over core).
Axes of the slice: x: 4, y: 4, z: 8, core: 2. Of those that a mesh axis runs over, the one named last changes fastest.
Arguments:
- query_input: bfloat16 [65536, 1536], P('seq', 'head'), may hold values from -400 to 400
- key_input: bfloat16 [65536, 1536], P('seq', 'head'), may hold values from -40 to 40
- value_input: bfloat16 [65536, 1536], P('seq', 'head'), may hold values from -60 to 60
- cube_lists: int32 [1024, 12, 32], P('seq', 'head'), may hold values from 0 to 1023, as said below
- coarse_gate: float32 [12], P('head'), may hold values from 0.5 to 2
- out_weight: bfloat16 [1536, 1536], replicated, may hold values from -0.875 to 0.875
Outputs:
- mixed_out: bfloat16 [65536, 1536], P('seq', 'head')
Inputs may be any that keep to these rules, and one draw needn't show every extreme that they name: `cube_lists`: A list holds 32 distinct cubes and never a cube of the query's own block of 8 cubes (the cubes of one index of seq). For each such block and each half of the heads, the distinct (head, key cube) pairs that the block's lists name among the cubes of one other block number at most 3; 3 is reached in every draw. Lists favour some blocks over others.
All inputs are finite; a program needn't handle non-finite values.
Results may differ from a plain program's by a relative error of at most 0.0054.
Values may be sent and summed in bfloat16 or wider, within the bound.
A program may use at most 128 MiB of HBM per device.

v0:
```python
import jax
import jax.numpy as jnp
from jax import lax
from jax.sharding import PartitionSpec as P


def slot_table(needed, slot_cap):
    unit_count = needed.shape[1]
    unit_rank = jnp.cumsum(needed.astype(jnp.int32), axis=1) - 1
    slot_iota = jnp.arange(slot_cap, dtype=jnp.int32)
    chosen = needed[:, :, None] & (unit_rank[:, :, None] == slot_iota[None, None, :])
    unit_iota = jnp.arange(unit_count, dtype=jnp.int32)
    slot_ids = jnp.sum(jnp.where(chosen, unit_iota[None, :, None], 0), axis=1)
    return (slot_ids, unit_rank)


def body(query_input, key_input, value_input, cube_lists, coarse_gate, out_weight):
    seq_count = lax.axis_size("seq")
    head_index = lax.axis_index("head")
    cube_count, heads_local, top_count = cube_lists.shape
    tok_count, local_width = query_input.shape
    cube_len = tok_count // cube_count
    head_dim = local_width // heads_local
    unit_count = heads_local * cube_count
    slot_cap = 2 * top_count * heads_local // seq_count
    score_scale = head_dim ** (-0.5)
    cube_shape = (cube_count, cube_len, heads_local, head_dim)
    query_cubes = query_input.reshape(cube_shape)
    key_cubes = key_input.reshape(cube_shape)
    value_cubes = value_input.reshape(cube_shape)
    pooled_q = jnp.mean(query_cubes.astype(jnp.float32), axis=1)
    pooled_k = jnp.mean(key_cubes.astype(jnp.float32), axis=1).reshape(cube_count, local_width)
    pooled_v = jnp.mean(value_cubes.astype(jnp.float32), axis=1).reshape(cube_count, local_width)
    all_keys, all_values = (
        lax.all_gather(pooled_k, "seq", axis=0, tiled=True),
        lax.all_gather(pooled_v, "seq", axis=0, tiled=True),
    )
    all_keys = all_keys.reshape(-1, heads_local, head_dim)
    all_values = all_values.reshape(-1, heads_local, head_dim)
    coarse_scores = (
        jnp.einsum("chd,nhd->chn", pooled_q, all_keys, precision=lax.Precision.HIGHEST)
        * score_scale
    )
    coarse_weights = jax.nn.softmax(coarse_scores, axis=-1).astype(jnp.bfloat16)
    coarse = jnp.einsum(
        "chn,nhd->chd",
        coarse_weights.astype(jnp.float32),
        all_values,
        precision=lax.Precision.HIGHEST,
    )
    owners = cube_lists // cube_count
    within = cube_lists % cube_count
    head_iota = jnp.arange(heads_local, dtype=jnp.int32)[None, :, None]
    unit_ids = head_iota * cube_count + within
    owner_flat = owners.reshape(-1)
    unit_flat = unit_ids.reshape(-1)
    needed_here = jnp.zeros((seq_count, unit_count), jnp.bool_).at[owner_flat, unit_flat].set(True)
    slot_ids, unit_rank = slot_table(needed_here, slot_cap)
    slot_of_entry = unit_rank[owner_flat, unit_flat]
    positions = (owner_flat * slot_cap + slot_of_entry).reshape(cube_lists.shape)
    key_units = jnp.transpose(key_cubes, (2, 0, 1, 3))
    value_units = jnp.transpose(value_cubes, (2, 0, 1, 3))
    kv_units = jnp.concatenate([key_units, value_units], axis=-1).reshape(
        unit_count, cube_len, 2 * head_dim
    )
    replied = kv_units[lax.all_to_all(slot_ids, "seq", split_axis=0, concat_axis=0, tiled=True)]
    fetched = lax.all_to_all(replied, "seq", split_axis=0, concat_axis=0, tiled=True)
    fetched_flat = fetched.reshape(seq_count * slot_cap, cube_len, 2 * head_dim)
    pair_count = 2

    def fine_block(block_index):
        row_start = block_index * pair_count
        block_q = lax.dynamic_slice_in_dim(query_cubes, row_start, pair_count, 0)
        block_k = lax.dynamic_slice_in_dim(key_cubes, row_start, pair_count, 0)
        block_v = lax.dynamic_slice_in_dim(value_cubes, row_start, pair_count, 0)
        block_pos = lax.dynamic_slice_in_dim(positions, row_start, pair_count, 0)
        remote = fetched_flat[block_pos]
        remote_k = remote[..., :head_dim]
        remote_v = remote[..., head_dim:]
        remote_scores = (
            jnp.einsum("bqhd,bhtkd->bhqtk", block_q, remote_k, preferred_element_type=jnp.float32)
            * score_scale
        )
        own_scores = (
            jnp.einsum("bqhd,bkhd->bhqk", block_q, block_k, preferred_element_type=jnp.float32)
            * score_scale
        )
        row_max = jnp.maximum(jnp.max(remote_scores, axis=(3, 4)), jnp.max(own_scores, axis=3))
        remote_exp = jnp.exp(remote_scores - row_max[..., None, None])
        own_exp = jnp.exp(own_scores - row_max[..., None])
        totals = jnp.sum(remote_exp, axis=(3, 4)) + jnp.sum(own_exp, axis=3)
        remote_w = (remote_exp / totals[..., None, None]).astype(jnp.bfloat16)
        own_w = (own_exp / totals[..., None]).astype(jnp.bfloat16)
        remote_part = jnp.einsum(
            "bhqtk,bhtkd->bqhd", remote_w, remote_v, preferred_element_type=jnp.float32
        )
        own_part = jnp.einsum("bhqk,bkhd->bqhd", own_w, block_v, preferred_element_type=jnp.float32)
        return remote_part + own_part

    fine_out = lax.map(fine_block, jnp.arange(cube_count // pair_count, dtype=jnp.int32)).reshape(
        cube_shape
    )
    attended = fine_out + coarse_gate[None, None, :, None] * coarse[:, None, :, :]
    attended = attended.astype(jnp.bfloat16).reshape(tok_count, local_width)
    weight_rows = lax.dynamic_slice_in_dim(out_weight, head_index * local_width, local_width, 0)
    partial_terms = jnp.dot(attended, weight_rows, preferred_element_type=jnp.float32)
    mixed_out = lax.psum_scatter(partial_terms, "head", scatter_dimension=1, tiled=True)
    return mixed_out.astype(jnp.bfloat16)


def solution(mesh):
    placed = (
        P("seq", "head"),
        P("seq", "head"),
        P("seq", "head"),
        P("seq", "head", None),
        P("head"),
        P(),
    )
    return jax.shard_map(
        body, mesh=mesh, in_specs=placed, out_specs=P("seq", "head"), check_vma=False
    )
```

profile of v0, /device:TPU:1, one launch (start us, length us, event | category | flops | bytes accessed | tf_op | source)
XLA Modules:
  0.0 569.2 jit_solution(11607551462509017840)
XLA Ops:
  9.1 11.2 %scatter_custom_fusion = pred[6144]{0:T(1024)(128)(4,1)S(1)} fusion(s32[1536]{0:T(1024)S(1)} %broadcast_select_fusion, pred[1536]{0:T(1024)(128)(4,1)S(1)} %broadcast.145, pred[]{:T(512)} %constant.80.clone.1), kind=kCustom, calls=%fused_computation.78 | custom fusion | bytes 6145
  21.2 16.5 %all-to-all-start = ((s32[128,1,3]{2,1,0:T(1,128)}), s32[128,1,3]{2,1,0:T(1,128)S(1)}, u32[]{:S(2)}, u32[]{:S(2)}) async-start(s32[128,1,3]{2,1,0:T(1,128)} %copy.79), calls=%async_computation | async-start | bytes 131072 | tf_op jit(solution)/shard_map/all_to_all | solution.py:66
  42.8 5.2 all-to-all-done
  48.3 11.3 %gather_fusion.2 = bf16[384,64,256]{2,1,0:T(8,128)(2,1)} fusion(bf16[48,64,256]{2,1,0:T(8,128)(2,1)S(1)} %bitcast.75, s32[1024]{0:T(1024)S(1)} %pad_clamp_fusion.1), kind=kCustom, calls=%fused_computation.2 | custom fusion | bytes 25167360 | tf_op jit(solution)/shard_map/gather | solution.py:66
  59.6 8.4 %all-to-all-start.1 = ((bf16[128,3,64,256]{3,2,1,0:T(8,128)(2,1)}), bf16[128,3,64,256]{3,2,1,0:T(8,128)(2,1)}, u32[]{:S(2)}, u32[]{:S(2)}) async-start(bf16[128,3,64,256]{3,2,1,0:T(8,128)(2,1)} %bitcast.76), calls=%async_computation.1 | async-start | bytes 25165824 | tf_op jit(solution)/shard_map/all_to_all | solution.py:67
  72.0 10.3 %gather_fusion.1 = s32[1536]{0:T(1024)S(1)} fusion(s32[128,48]{0,1:T(8,128)S(1)} %broadcast_add_fusion, s32[1536]{0:T(1024)S(1)} %get-tuple-element.102), kind=kCustom, calls=%fused_computation.1 | custom fusion | bytes 24576 | tf_op jit(solution)/shard_map/gather | solution.py:59
  84.6 140.3 %all-gather.5.cloned.1.call-done = f32[1024,768]{1,0:T(8,128)} async-done(((f32[8,768]{1,0:T(8,128)}), f32[1024,768]{1,0:T(8,128)}) %all-gather.5.cloned.1.call-update) | async-done | bytes 3145744 | tf_op jit(solution)/shard_map/all_gather | solution.py:35
  225.0 3.5 copy.85
  228.5 144.8 %all-gather.3.cloned.1.call-done = f32[1024,768]{1,0:T(8,128)} async-done(((f32[8,768]{1,0:T(8,128)}), f32[1024,768]{1,0:T(8,128)}) %all-gather.3.cloned.1.call-update) | async-done | bytes 3145744 | tf_op jit(solution)/shard_map/all_gather | solution.py:36
  373.3 2.4 copy.84
  375.7 3.6 fusion.28
  382.5 153.4 %while.10 = (s32[]{:T(128)}, f32[4,2,64,6,128]{4,2,3,1,0:T(8,128)}, s32[4]{0:T(128)S(1)}, s32[8,6,32]{2,1,0:T(8,128)S(1)}, bf16[384,64,256]{2,1,0:T(8,128)(2,1)}...) while((s32[]{:T(128)}, f32[4,2,64,6,128]{4,2,3,1,0:T(8,128)}, ...), condition=%wide.region_8.9_spmd, body=%wide.region_3.8_spmd.sunk | while | flops 845070976 | bytes 90700000 | solution.py:100
  385.1 15.8 %gather_fusion = bf16[384,64,256]{2,1,0:T(8,128)(2,1)} fusion(bf16[384,64,256]{2,1,0:T(8,128)(2,1)} %get-tuple-element.192, s32[1024]{0:T(1024)S(1)} %pad_clamp_fusion.3), kind=kCustom, calls=%fused_computation.clone.1 | custom fusion | bytes 25167360 | tf_op jit(solution)/shard_map/while/body/eval_jaxpr/gather | solution.py:77
  401.0 4.1 multiply_reduce_fusion.3
  405.2 2.5 fusion.56
  409.7 9.2 %fusion.58 = f32[2,6,128,64]{2,3,1,0:T(8,128)S(1)} fusion(f32[2,6,64,32,64]{2,4,3,1,0:T(8,128)} %copy-done, f32[2,6,64]{2,1,0:T(8,128)S(1)} %add.157, f32[2,6,64]{2,1,0:T(8,128)S(1)} %max.14, bf16[2,6,32,64,256]{4,3,2,1,0:T(8,128)(2,1)} %bitcast.74), kind=kOutput, calls=%fused_computation.16.clone.1 | convolution fusion | flops 408944640 | bytes 19273728 | tf_op jit(solution)/shard_map/while/body/eval_jaxpr/bhqtk,bhtkd->bqhd/dot_general | solution.py:94
  423.5 15.8 %gather_fusion = bf16[384,64,256]{2,1,0:T(8,128)(2,1)} fusion(bf16[384,64,256]{2,1,0:T(8,128)(2,1)} %get-tuple-element.192, s32[1024]{0:T(1024)S(1)} %pad_clamp_fusion.3), kind=kCustom, calls=%fused_computation.clone.1 | custom fusion | bytes 25167360 | tf_op jit(solution)/shard_map/while/body/eval_jaxpr/gather | solution.py:77
  439.3 4.1 multiply_reduce_fusion.3
  443.6 2.5 fusion.56
  448.0 9.2 %fusion.58 = f32[2,6,128,64]{2,3,1,0:T(8,128)S(1)} fusion(f32[2,6,64,32,64]{2,4,3,1,0:T(8,128)} %copy-done, f32[2,6,64]{2,1,0:T(8,128)S(1)} %add.157, f32[2,6,64]{2,1,0:T(8,128)S(1)} %max.14, bf16[2,6,32,64,256]{4,3,2,1,0:T(8,128)(2,1)} %bitcast.74), kind=kOutput, calls=%fused_computation.16.clone.1 | convolution fusion | flops 408944640 | bytes 19273728 | tf_op jit(solution)/shard_map/while/body/eval_jaxpr/bhqtk,bhtkd->bqhd/dot_general | solution.py:94
  461.8 15.8 %gather_fusion = bf16[384,64,256]{2,1,0:T(8,128)(2,1)} fusion(bf16[384,64,256]{2,1,0:T(8,128)(2,1)} %get-tuple-element.192, s32[1024]{0:T(1024)S(1)} %pad_clamp_fusion.3), kind=kCustom, calls=%fused_computation.clone.1 | custom fusion | bytes 25167360 | tf_op jit(solution)/shard_map/while/body/eval_jaxpr/gather | solution.py:77
  477.7 4.1 multiply_reduce_fusion.3
  481.9 2.5 fusion.56
  486.4 9.2 %fusion.58 = f32[2,6,128,64]{2,3,1,0:T(8,128)S(1)} fusion(f32[2,6,64,32,64]{2,4,3,1,0:T(8,128)} %copy-done, f32[2,6,64]{2,1,0:T(8,128)S(1)} %add.157, f32[2,6,64]{2,1,0:T(8,128)S(1)} %max.14, bf16[2,6,32,64,256]{4,3,2,1,0:T(8,128)(2,1)} %bitcast.74), kind=kOutput, calls=%fused_computation.16.clone.1 | convolution fusion | flops 408944640 | bytes 19273728 | tf_op jit(solution)/shard_map/while/body/eval_jaxpr/bhqtk,bhtkd->bqhd/dot_general | solution.py:94
  500.2 15.8 %gather_fusion = bf16[384,64,256]{2,1,0:T(8,128)(2,1)} fusion(bf16[384,64,256]{2,1,0:T(8,128)(2,1)} %get-tuple-element.192, s32[1024]{0:T(1024)S(1)} %pad_clamp_fusion.3), kind=kCustom, calls=%fused_computation.clone.1 | custom fusion | bytes 25167360 | tf_op jit(solution)/shard_map/while/body/eval_jaxpr/gather | solution.py:77
  516.0 4.1 multiply_reduce_fusion.3
  520.3 2.5 fusion.56
  524.7 9.2 %fusion.58 = f32[2,6,128,64]{2,3,1,0:T(8,128)S(1)} fusion(f32[2,6,64,32,64]{2,4,3,1,0:T(8,128)} %copy-done, f32[2,6,64]{2,1,0:T(8,128)S(1)} %add.157, f32[2,6,64]{2,1,0:T(8,128)S(1)} %max.14, bf16[2,6,32,64,256]{4,3,2,1,0:T(8,128)(2,1)} %bitcast.74), kind=kOutput, calls=%fused_computation.16.clone.1 | convolution fusion | flops 408944640 | bytes 19273728 | tf_op jit(solution)/shard_map/while/body/eval_jaxpr/bhqtk,bhtkd->bqhd/dot_general | solution.py:94
  535.9 2.5 copy.83
  538.7 3.2 fusion.23
  541.9 18.4 %reduce-scatter.2.cloned.1.call-done = f32[512,768]{1,0:T(8,128)} async-done(((f32[512,1536]{1,0:T(8,128)}), f32[512,768]{1,0:T(8,128)}) %reduce-scatter.2.cloned.1.call-update) | async-done | bytes 1572880 | tf_op jit(solution)/shard_map/reduce_scatter | solution.py:107
  560.3 2.4 convert_element_type.35
  (106 shorter events, 42.6 us)
Async XLA Ops:
  21.2 26.8 %all-to-all-start = ((s32[128,1,3]{2,1,0:T(1,128)}), s32[128,1,3]{2,1,0:T(1,128)S(1)}, u32[]{:S(2)}, u32[]{:S(2)}) async-start(s32[128,1,3]{2,1,0:T(1,128)} %copy.79), calls=%async_computation | async-start | bytes 131072 | tf_op jit(solution)/shard_map/all_to_all | solution.py:66
  39.7 2.3 copy-start.1
  59.5 8.4 %copy-start.2 = (bf16[8,64,6,128]{3,2,1,0:T(8,128)(2,1)S(1)}, bf16[8,64,6,128]{3,2,1,0:T(8,128)(2,1)}, u32[]{:S(2)}) copy-start(bf16[8,64,6,128]{3,2,1,0:T(8,128)(2,1)} %copy-done.1) | copy-start | bytes 2359300
  59.6 322.9 %all-to-all-start.1 = ((bf16[128,3,64,256]{3,2,1,0:T(8,128)(2,1)}), bf16[128,3,64,256]{3,2,1,0:T(8,128)(2,1)}, u32[]{:S(2)}, u32[]{:S(2)}) async-start(bf16[128,3,64,256]{3,2,1,0:T(8,128)(2,1)} %bitcast.76), calls=%async_computation.1 | async-start | bytes 25165824 | tf_op jit(solution)/shard_map/all_to_all | solution.py:67
  67.9 157.0 %all-gather.5.cloned.1.call-start = ((), (), s32[]{:S(2)}) async-start(), calls=%async_computation.4 | async-start | bytes 3170304 | tf_op jit(solution)/shard_map/all_gather | solution.py:35
  68.9 304.4 %all-gather.3.cloned.1.call-start = ((), (), s32[]{:S(2)}) async-start(), calls=%async_computation.3 | async-start | bytes 3170304 | tf_op jit(solution)/shard_map/all_gather | solution.py:36
  69.8 490.6 %reduce-scatter.2.cloned.1.call-start = ((), (), s32[]{:S(2)}) async-start(), calls=%async_computation.5 | async-start | bytes 4718592 | tf_op jit(solution)/shard_map/reduce_scatter | solution.py:107
  72.0 10.4 %copy-start.4 = (bf16[512,768]{1,0:T(8,128)(2,1)S(1)}, bf16[512,768]{1,0:T(8,128)(2,1)}, u32[]{:S(2)}) copy-start(bf16[512,768]{1,0:T(8,128)(2,1)} %param.8) | copy-start | bytes 2359300
  82.3 2.3 copy-start.6
  228.5 151.8 %copy-start.7 = (f32[6]{0:T(128)S(1)}, f32[6]{0:T(128)}, u32[]{:S(2)}) copy-start(f32[6]{0:T(128)} %param.12) | copy-start | bytes 76
  382.5 155.9 %copy-start.5 = (f32[8,6,128]{2,1,0:T(8,128)S(1)}, f32[8,6,128]{2,1,0:T(8,128)}, u32[]{:S(2)}) copy-start(f32[8,6,128]{2,1,0:T(8,128)} %copy.89) | copy-start | bytes 73732
  405.1 4.6 copy-start
  443.5 4.6 copy-start
  481.8 4.6 copy-start
  520.1 4.6 copy-start
  535.9 2.8 copy-start.3
Sparse Core Ops, SparseCore 0:
  72.5 152.4 all-gather.4
  228.6 144.5 all-gather.2
  542.0 18.2 reduce-scatter.1
where the time goes:
time: 570 us; the launch traced here: 569 us
  waiting for transfers between devices  309 us (54%)
  local copies, waits for them, and re-layouts  127 us (22%)
  matrix products  74.5 us (13%)
  starting transfers between devices  25 us (4%)
  other arithmetic  17.3 us (3%)
  between operations  13.4 us (2%)
    all_gather x1, waiting for transfers between devices, body(): lax.all_gather(pooled_v, 'seq', axis=0, tiled=True)  145 us
    all_gather x1, waiting for transfers between devices, body(): lax.all_gather(pooled_k, 'seq', axis=0, tiled=True)  140 us
    gather x4, local copies, waits for them, and re-layouts, fine_block(): remote = fetched_flat[block_pos]  63.4 us
    dot_general x4, matrix products, fine_block(): jnp.einsum('bhqtk,bhtkd->bqhd', remote_w, remote_v, preferred_element_typ...  36.9 us
    reduce_scatter x1, waiting for transfers between devices, body(): lax.psum_scatter(partial_terms, 'head', scatter_dimension=1, tiled=True)  18.4 us
    all_to_all x1, starting transfers between devices, body(): lax.all_to_all(slot_ids, 'seq', split_axis=0, concat_axis=0, tiled=True)  16.5 us
    dot_general x4, matrix products, fine_block(): jnp.einsum('bqhd,bhtkd->bhqtk', block_q, remote_k, preferred_element_type...  16.5 us
    unnamed x18, local copies, waits for them, and re-layouts  12.7 us
  transfers between devices with their start and end apart: 5, of which 4 were waited for; matrix products, arithmetic and copies ran while one was open for 6% of the time, Pallas kernels for 0%

commit v1 on v0

v1 whole, which is shorter than its diff:
```python
import functools

import jax
import jax.numpy as jnp
from jax import lax
from jax.experimental import pallas as pl
from jax.experimental.pallas import tpu as pltpu
from jax.sharding import PartitionSpec as P

NX, NY, NZ = 4, 4, 8
PLANE = NX * NY
SLOTS = 3
CUBES = 8
HEADS = 6
TOK = 64
HD = 128
TOP = 32
UNITS = CUBES * HEADS
MAXU = 224
GROUP = 16
RING = MAXU // GROUP + 1
NEG = -1e30
AHEAD = 4
PACK = SLOTS * TOK
SCALE = HD ** -0.5
LOG2E = 1.4426950408889634
NT = (((1,), (1,)), ((), ()))


def iota(shape, dim):
    return lax.broadcasted_iota(jnp.int32, shape, dim)


def flag(mask):
    return jnp.where(mask, 1.0, 0.0).astype(jnp.bfloat16)


def unit_slots(lists_ref, table_ref, bits_ref, rank_ref):
    entry_bit = 1 << (iota((CUBES, 256), 1) >> 5)
    bits = []
    for h in range(HEADS):
        row = lists_ref[h:h + 1, :]
        owner_hot = flag((row >> 3) == iota((128, 256), 0))
        within_bit = jnp.where((row & 7) == iota((CUBES, 256), 0), entry_bit, 0)
        bits.append(lax.dot_general(within_bit.astype(jnp.float32).astype(jnp.bfloat16), owner_hot, NT,
                                    preferred_element_type=jnp.float32))
    bits = jnp.concatenate(bits, axis=0)
    need = bits > 0
    lower = flag(iota((UNITS, UNITS), 0) >= iota((UNITS, UNITS), 1))
    rank = jnp.dot(lower, flag(need), preferred_element_type=jnp.float32)
    bits_ref[...] = bits
    rank_ref[...] = rank
    unit = iota((UNITS, 128), 0)
    table_ref[...] = jnp.zeros_like(table_ref)
    for s in range(SLOTS):
        table_ref[s:s + 1, :] = jnp.sum(jnp.where(need & (rank == s + 1), unit, 0), axis=0, keepdims=True)


def head_lists(bits_ref, rank_ref, count_ref, slots_ref, cubes_ref):
    bits, rank = bits_ref[...], rank_ref[...]
    need = bits > 0
    mine, mine_bits = [], []
    for s in range(SLOTS):
        hit = jnp.where(need & (rank == s + 1), 1.0, 0.0)
        seen = hit * bits
        mine.append([jnp.sum(hit[h * 8:h * 8 + 8], axis=0, keepdims=True) for h in range(HEADS)])
        mine_bits.append([jnp.sum(seen[h * 8:h * 8 + 8], axis=0, keepdims=True) for h in range(HEADS)])
    wide = SLOTS * 128
    upper = flag(iota((wide, wide), 0) <= iota((wide, wide), 1))
    lane = iota((1, wide), 1)
    owner = lane & 127
    place = ((owner >> 5) * NX + (owner & 3)) * NZ + ((owner >> 2) & 7)
    place = jnp.broadcast_to(place.astype(jnp.float32), (8, wide))
    slot = jnp.broadcast_to((lane >> 7).astype(jnp.float32), (8, wide))
    sub = iota((8, wide), 0)
    for h in range(HEADS):
        have = jnp.concatenate([mine[s][h] for s in range(SLOTS)], axis=1)
        have_bits = jnp.concatenate([mine_bits[s][h] for s in range(SLOTS)], axis=1)
        have8 = jnp.broadcast_to(have, (8, wide))
        order = jnp.dot(have8.astype(jnp.bfloat16), upper, preferred_element_type=jnp.float32)
        want = (iota((256, wide), 0) + 1).astype(jnp.float32)
        hit = jnp.where((order[0:1, :] == want) & (have > 0), 1.0, 0.0).astype(jnp.bfloat16)
        facts = jnp.where(sub == 0, place, jnp.where(sub == 1, slot, jnp.broadcast_to(have_bits, (8, wide))))
        facts = lax.dot_general(facts.astype(jnp.bfloat16), hit, NT, preferred_element_type=jnp.float32)
        slots_ref[h:h + 1, :] = (facts[0:1, :] * SLOTS + facts[1:2, :]).astype(jnp.int32)
        cubes_ref[h:h + 1, :] = facts[2:3, :].astype(jnp.int32)
        total = jnp.sum(have, axis=1, keepdims=True)
        count_ref[h:h + 1, :] = jnp.broadcast_to(total, (1, 128)).astype(jnp.int32)


def exchange(
    q_hbm, k_hbm, v_hbm, lists_ref, recv, coarse_ref, count_ref, slots_ref, cubes_ref, *scratch
):
    q_own = scratch[0]
    kk = scratch[1:9]
    vv = scratch[9:17]
    (send_buf, tbl_ref, bits_ref, rank_ref, tbl_all, tbl_sm, q_all, pool_k, pool_v, o_res, o_half, o_got, stats, stats_all,
     load_sem, z_send, z_recv, t_send, t_recv, q_send, q_recv, u_send, u_recv,
     o_send, o_recv, m_send, m_recv, sm_sem, loc_sem) = scratch[17:]
    s = lax.axis_index("seq")
    x = lax.rem(s, NX)
    z = lax.rem(lax.div(s, NX), NZ)
    y = lax.div(s, NX * NZ)
    me = y * NX + x

    def peer(j):
        px = lax.rem(x + lax.rem(j, NX), NX)
        py = lax.rem(y + lax.div(j, NX), NY)
        return py * NX + px, (py * NZ + z) * NX + px

    def remote(src, dst, send, recv_, seq):
        return pltpu.make_async_remote_copy(
            src_ref=src, dst_ref=dst, send_sem=send, recv_sem=recv_,
            device_id={"seq": seq}, device_id_type=pl.DeviceIdType.MESH,
        )

    right = (y * NZ + lax.rem(z + 1, NZ)) * NX + x
    left = (y * NZ + lax.rem(z + NZ - 1, NZ)) * NX + x

    loads = []
    for i, (src, dst) in enumerate(((k_hbm, kk[0]), (v_hbm, vv[0]), (q_hbm, q_own))):
        for h in range(HEADS):
            loads.append(pltpu.make_async_copy(
                src.at[:, :, pl.ds(h * HD, HD)], dst.at[pl.ds(h * CUBES, CUBES)], load_sem.at[i * HEADS + h]))
    for c in loads:
        c.start()

    barrier = pltpu.get_barrier_semaphore()
    for seq in (right, left):
        pl.semaphore_signal(barrier, inc=1, device_id={"seq": seq}, device_id_type=pl.DeviceIdType.MESH)

    @pl.loop(1, PLANE)
    def _(j):
        pl.semaphore_signal(barrier, inc=1, device_id={"seq": peer(j)[1]}, device_id_type=pl.DeviceIdType.MESH)

    unit_slots(lists_ref, tbl_ref, bits_ref, rank_ref)
    pl.semaphore_wait(barrier, PLANE + 1)

    @pl.loop(1, PLANE)
    def _(j):
        pp, seq = peer(j)
        remote(tbl_ref, tbl_all.at[me], t_send.at[j], t_recv.at[me], seq).start()

    def ring(first, second, base, far, seq, sem0):
        out = []
        for n in range(14):
            vals = first if n % 4 < 2 else second
            stage = n // 4
            src = vals[0 if stage == 0 else base + stage - 1]
            dst = vals[base + stage if stage < 3 else far]
            part = pl.ds((n % 2) * 24, 24)
            out.append(remote(src.at[part], dst.at[part], z_send.at[sem0 + n], z_recv.at[sem0 + n], seq))
        return out

    to_right = ring(kk, vv, 1, 7, right, 0)
    to_left = ring(vv, kk, 4, 7, left, 14)

    for c in loads[:2 * HEADS]:
        c.wait()
    for n in range(AHEAD):
        to_right[n].start()
        to_left[n].start()

    tbl_all[me] = tbl_ref[...]
    for c in loads[2 * HEADS:]:
        c.wait()

    row = lax.broadcasted_iota(jnp.int32, (CUBES, 512), 0)
    col = lax.broadcasted_iota(jnp.int32, (CUBES, 512), 1)
    mean = jnp.where(lax.div(col, TOK) == row, 1.0 / TOK, 0.0).astype(jnp.bfloat16)

    @pl.loop(0, HEADS)
    def _(h):
        q_all[me, pl.ds(h * CUBES, CUBES), :] = jnp.dot(
            mean, q_own[pl.ds(h * CUBES, CUBES)].reshape(512, HD), preferred_element_type=jnp.float32)

    @pl.loop(1, PLANE)
    def _(j):
        pp, seq = peer(j)
        remote(q_all.at[me], q_all.at[me], q_send.at[j], q_recv.at[me], seq).start()

    @pl.loop(1, PLANE)
    def _(j):
        pp, seq = peer(j)
        remote(tbl_ref, tbl_all.at[pp], t_send.at[j], t_recv.at[pp], seq).wait()

    to_smem = pltpu.make_async_copy(tbl_all, tbl_sm, sm_sem)
    to_smem.start()
    to_smem.wait()

    def owner_z(k):
        if k <= 3:
            return lax.rem(z + NZ - k, NZ)
        if k <= 6:
            return lax.rem(z + k - 3, NZ)
        return lax.rem(z + 4, NZ)

    def pick(k, val, pp):
        lane = (y * NZ + owner_z(k)) * NX + x
        src = vv[k] if val else kk[k]
        for sl in range(SLOTS):
            send_buf[val, k, pp, pl.ds(sl * TOK, TOK), :] = src[jnp.clip(tbl_sm[pp, sl, lane], 0, UNITS - 1)]

    def own_copy(k, val):
        return pltpu.make_async_copy(send_buf.at[val, k, me], recv.at[val, me * NZ + owner_z(k)], loc_sem.at[val, k])

    def handle(k, val):
        oz = owner_z(k)

        @pl.loop(1, PLANE)
        def _(j):
            pp, seq = peer(j)
            pick(k, val, pp)
            remote(send_buf.at[val, k, pp], recv.at[val, me * NZ + oz],
                   u_send.at[val, k, j], u_recv.at[val, oz, me], seq).start()

        if k > 0:
            pick(k, val, me)
            own_copy(k, val).start()

    def pool(k, val):
        src, dst = (vv[k], pool_v) if val else (kk[k], pool_k)

        @pl.loop(0, HEADS)
        def _(h):
            dst[h, pl.ds(k * CUBES, CUBES), :] = jnp.dot(
                mean, src[pl.ds(h * CUBES, CUBES)].reshape(512, HD), preferred_element_type=jnp.float32)

    handle(0, 0)
    handle(0, 1)
    pool(0, 0)
    pool(0, 1)
    head_lists(bits_ref, rank_ref, count_ref, slots_ref, cubes_ref)
    for n in range(14):
        for way in (to_right, to_left):
            way[n].wait_recv()
            if n + AHEAD < 14:
                way[n + AHEAD].start()
        if n % 2:
            stage = n // 4
            val = (n % 4) // 2
            for k, which in ((1 + stage if stage < 3 else 7, val), (4 + stage if stage < 3 else 7, 1 - val)):
                if stage < 3:
                    handle(k, which)
                pool(k, which)

    @pl.loop(1, PLANE)
    def _(j):
        pp, seq = peer(j)
        remote(q_all.at[me], q_all.at[pp], q_send.at[j], q_recv.at[pp], seq).wait()

    lane3 = lax.broadcasted_iota(jnp.int32, (PLANE * CUBES, HD), 1)

    def coarse_head(h, stat):
        rows = pl.ds(pl.multiple_of(h * CUBES, CUBES), CUBES)
        qh = q_all[:, rows, :].reshape(PLANE * CUBES, HD)
        sc = lax.dot_general(qh, pool_k[h], NT, precision=lax.Precision.HIGHEST,
                             preferred_element_type=jnp.float32) * SCALE
        top = jnp.max(sc, axis=1, keepdims=True)
        e = jnp.exp(sc - top)
        tot = jnp.sum(e, axis=1, keepdims=True)
        o = jnp.dot(e, pool_v[h], precision=lax.Precision.HIGHEST, preferred_element_type=jnp.float32)
        o_res[:, rows, :] = o.reshape(PLANE, CUBES, HD)
        stat = jnp.where(lane3 == h, top, stat)
        return jnp.where(lane3 == h + 64, tot, stat)

    stat = lax.fori_loop(0, HEADS, coarse_head, jnp.zeros((PLANE * CUBES, HD), jnp.float32))
    stats[...] = stat.reshape(PLANE, CUBES, HD)
    o_half[...] = o_res[...].astype(jnp.bfloat16)

    @pl.loop(1, PLANE)
    def _(j):
        pp, seq = peer(j)
        remote(o_half.at[pp], o_got.at[me], o_send.at[j], o_recv.at[me], seq).start()
        remote(stats.at[pp], stats_all.at[me], m_send.at[j], m_recv.at[me], seq).start()

    handle(7, 0)
    handle(7, 1)
    o_got[me] = o_half[me]
    stats_all[me] = stats[me]

    @pl.loop(1, PLANE)
    def _(j):
        pp, seq = peer(j)
        remote(o_half.at[pp], o_got.at[pp], o_send.at[j], o_recv.at[pp], seq).wait()
        remote(stats.at[pp], stats_all.at[pp], m_send.at[j], m_recv.at[pp], seq).wait()

    o_res[...] = o_got[...].astype(jnp.float32)
    for h in range(HEADS):
        top = stats_all[:, :, h:h + 1]
        tot = stats_all[:, :, 64 + h:65 + h]
        w = jnp.exp(top - jnp.max(top, axis=0, keepdims=True))
        den = jnp.sum(w * tot, axis=0)
        num = jnp.sum(w * o_res[:, pl.ds(h * CUBES, CUBES), :], axis=0)
        coarse_ref[pl.ds(h * CUBES, CUBES), :] = num / den

    for c in to_right + to_left:
        c.wait_send()
    for k in range(NZ):
        oz = owner_z(k)
        for val in range(2):
            if k > 0:
                own_copy(k, val).wait()

            @pl.loop(1, PLANE)
            def _(j):
                pp, seq = peer(j)
                remote(send_buf.at[val, k, pp], recv.at[val, pp * NZ + oz],
                       u_send.at[val, k, j], u_recv.at[val, oz, pp], seq).wait()


def fine(count_ref, slot_ref, bits_ref, gate_ref, q_ref, k_ref, v_ref, coarse_ref, recv_hbm, out_ref,
         recv, s_buf, s_own, top, peak, tot, acc, sem):
    c2 = SCALE * LOG2E
    pairs = GROUP // 2
    copies = [pltpu.make_async_copy(recv_hbm.at[i], recv.at[i], sem.at[i]) for i in range(2)]
    for c in copies:
        c.start()
    same = (lax.broadcasted_iota(jnp.int32, (128, 128), 0) < TOK) == (
        lax.broadcasted_iota(jnp.int32, (128, 128), 1) < TOK)
    lane = lax.broadcasted_iota(jnp.int32, (1, 128), 1)

    def columns(h):
        return pl.ds(pl.multiple_of(h * HD, HD), HD)

    def blocks(h):
        return lax.div(count_ref[jnp.minimum(h, HEADS - 1), 0] + GROUP - 1, GROUP)

    def step(at):
        h, g = at
        last = g + 1 >= blocks(h)
        return jnp.where(last, h + 1, h), jnp.where(last, 0, g + 1)

    def units(val, h, g):
        return jnp.concatenate(
            [recv[val, slot_ref[h, jnp.minimum(g * GROUP + t, count_ref[h, 0] - 1)]] for t in range(GROUP)], axis=0)

    def score(i, at):
        h, g = at
        slot = lax.rem(i, RING)
        sc = lax.dot_general(q_ref[:, columns(h)], units(0, h, g), NT, preferred_element_type=jnp.float32)
        rowbits = [
            jnp.where(lane < TOK, bits_ref[h, g * GROUP + 2 * t], bits_ref[h, g * GROUP + 2 * t + 1])
            for t in range(pairs)
        ]
        for c in range(CUBES):
            rows = pl.ds(c * TOK, TOK)
            best = top[h, rows, :]
            for t in range(pairs):
                bias = jnp.where((rowbits[t] >> c) & 1 == 1, 0.0, NEG)
                part = sc[c * TOK:(c + 1) * TOK, t * 128:(t + 1) * 128] + bias
                s_buf[slot, t, rows, :] = part
                best = jnp.maximum(best, part)
            top[h, rows, :] = best

    def begin(at):
        h, g = at

        @pl.when(g == 0)
        def _():
            peak[...] = jnp.broadcast_to(jnp.max(top[h], axis=1, keepdims=True) * c2, (CUBES * TOK, HD))
            for c in range(CUBES // 2):
                rows = pl.ds(c * 128, 128)
                e = jnp.exp2(s_own[h, rows, :] * c2 - peak[rows, :])
                tot[rows, :] = e
                acc[rows, :] = jnp.dot(
                    e.astype(jnp.bfloat16), v_ref[rows, columns(h)], preferred_element_type=jnp.float32)

    def value(i, at):
        h, g = at
        slot = lax.rem(i, RING)
        blocks_of_rows = []
        for c in range(CUBES):
            rows = pl.ds(c * TOK, TOK)
            high, sums, parts = peak[rows, :], tot[rows, :], []
            for t in range(pairs):
                e = jnp.exp2(s_buf[slot, t, rows, :] * c2 - high)
                sums += e
                parts.append(e.astype(jnp.bfloat16))
            tot[rows, :] = sums
            blocks_of_rows.append(jnp.concatenate(parts, axis=1))
        acc[...] += jnp.dot(
            jnp.concatenate(blocks_of_rows, axis=0), units(1, h, g), preferred_element_type=jnp.float32)

    def finish(at):
        h, g = at

        @pl.when(g + 1 == blocks(h))
        def _():
            for c in range(CUBES):
                rows = pl.ds(c * TOK, TOK)
                total = jnp.sum(tot[rows, :], axis=1, keepdims=True)
                pooled = gate_ref[h] * coarse_ref[pl.ds(h * CUBES + c, 1), :]
                out_ref[rows, columns(h)] = (acc[rows, :] / total + pooled).astype(jnp.bfloat16)

    @pl.loop(0, HEADS)
    def _(h):
        for c in range(CUBES // 2):
            rows = pl.ds(c * 128, 128)
            sc = lax.dot_general(
                q_ref[rows, columns(h)], k_ref[rows, columns(h)], NT, preferred_element_type=jnp.float32)
            sc = jnp.where(same, sc, NEG)
            s_own[h, rows, :] = sc
            top[h, rows, :] = sc

    longest, items = blocks(0), blocks(0)
    for h in range(1, HEADS):
        longest, items = jnp.maximum(longest, blocks(h)), items + blocks(h)
    copies[0].wait()

    def only_score(i, at):
        score(i, at)
        return step(at)

    def both(i, carry):
        ahead, at = carry
        begin(at)
        value(i - longest, at)
        score(i, ahead)
        finish(at)
        return step(ahead), step(at)

    def only_value(i, at):
        begin(at)
        value(i - longest, at)
        finish(at)
        return step(at)

    zero = jnp.int32(0)
    ahead = lax.fori_loop(0, longest, only_score, (zero, zero))
    copies[1].wait()
    ahead, at = lax.fori_loop(longest, items, both, (ahead, (zero, zero)))
    lax.fori_loop(items, items + longest, only_value, at)


def project(att_ref, w_hbm, out_ref, other, w_buf, total, send_sem, recv_sem, w_sem):
    head = lax.axis_index("head")
    width = HEADS * HD
    weights = pltpu.make_async_copy(w_hbm.at[:, pl.ds(pl.multiple_of(head * width, width), width)], w_buf, w_sem)
    weights.start()
    barrier = pltpu.get_barrier_semaphore()
    pl.semaphore_signal(barrier, inc=1, device_id={"head": 1 - head}, device_id_type=pl.DeviceIdType.MESH)
    pl.semaphore_wait(barrier, 1)
    swap = pltpu.make_async_remote_copy(
        src_ref=att_ref, dst_ref=other, send_sem=send_sem, recv_sem=recv_sem,
        device_id={"head": 1 - head}, device_id_type=pl.DeviceIdType.MESH)
    swap.start()
    weights.wait()
    mine = pl.ds(pl.multiple_of(head * width, width), width)
    theirs = pl.ds(pl.multiple_of((1 - head) * width, width), width)
    total[...] = jnp.dot(att_ref[...], w_buf[mine, :], preferred_element_type=jnp.float32)
    swap.wait()
    out_ref[...] = (
        total[...] + jnp.dot(other[...], w_buf[theirs, :], preferred_element_type=jnp.float32)).astype(jnp.bfloat16)


def body(query_input, key_input, value_input, cube_lists, coarse_gate, out_weight):
    lists = jnp.transpose(cube_lists, (1, 0, 2)).reshape(HEADS, CUBES * TOP)
    any_spec = pl.BlockSpec(memory_space=pl.ANY)
    vmem_spec = pl.BlockSpec(memory_space=pltpu.VMEM)
    smem_spec = pl.BlockSpec(memory_space=pltpu.SMEM)
    dma = pltpu.SemaphoreType.DMA
    recv, coarse, count, slots, cubes = pl.pallas_call(
        exchange,
        out_shape=(
            jax.ShapeDtypeStruct((2, PLANE * NZ, PACK, HD), jnp.bfloat16),
            jax.ShapeDtypeStruct((UNITS, HD), jnp.float32),
            jax.ShapeDtypeStruct((HEADS, 128), jnp.int32),
            jax.ShapeDtypeStruct((HEADS, 256), jnp.int32),
            jax.ShapeDtypeStruct((HEADS, 256), jnp.int32),
        ),
        in_specs=[any_spec] * 3 + [vmem_spec],
        out_specs=(any_spec,) + (vmem_spec,) * 4,
        scratch_shapes=[pltpu.VMEM((UNITS, TOK, HD), jnp.bfloat16)] * 17 + [
            pltpu.VMEM((2, NZ, PLANE, PACK, HD), jnp.bfloat16),
            pltpu.VMEM((8, 128), jnp.int32),
            pltpu.VMEM((UNITS, 128), jnp.float32),
            pltpu.VMEM((UNITS, 128), jnp.float32),
            pltpu.VMEM((PLANE, 8, 128), jnp.int32),
            pltpu.SMEM((PLANE, 8, 128), jnp.int32),
            pltpu.VMEM((PLANE, UNITS, HD), jnp.float32),
            pltpu.VMEM((HEADS, NZ * CUBES, HD), jnp.float32),
            pltpu.VMEM((HEADS, NZ * CUBES, HD), jnp.float32),
            pltpu.VMEM((PLANE, UNITS, HD), jnp.float32),
            pltpu.VMEM((PLANE, UNITS, HD), jnp.bfloat16),
            pltpu.VMEM((PLANE, UNITS, HD), jnp.bfloat16),
            pltpu.VMEM((PLANE, CUBES, HD), jnp.float32),
            pltpu.VMEM((PLANE, CUBES, HD), jnp.float32),
            dma((18,)), dma((28,)), dma((28,)), dma((PLANE,)), dma((PLANE,)), dma((PLANE,)), dma((PLANE,)),
            dma((2, NZ, PLANE)), dma((2, NZ, PLANE)), dma((PLANE,)), dma((PLANE,)), dma((PLANE,)), dma((PLANE,)), dma, dma((2, NZ)),
        ],
        compiler_params=pltpu.CompilerParams(
            collective_id=0, has_side_effects=True, vmem_limit_bytes=56 * 1024 * 1024),
        name="exchange",
    )(*[t.reshape(CUBES, TOK, HEADS * HD) for t in (query_input, key_input, value_input)], lists)
    attended = pl.pallas_call(
        fine,
        out_shape=jax.ShapeDtypeStruct((CUBES * TOK, HEADS * HD), jnp.bfloat16),
        in_specs=[smem_spec] * 4 + [vmem_spec] * 4 + [any_spec],
        out_specs=vmem_spec,
        scratch_shapes=[
            pltpu.VMEM((2, PLANE * NZ * SLOTS, TOK, HD), jnp.bfloat16),
            pltpu.VMEM((RING, GROUP // 2, CUBES * TOK, HD), jnp.float32),
        ] + [pltpu.VMEM((HEADS, CUBES * TOK, HD), jnp.float32)] * 2 + [pltpu.VMEM((CUBES * TOK, HD), jnp.float32)] * 3
        + [dma((2,))],
        compiler_params=pltpu.CompilerParams(vmem_limit_bytes=56 * 1024 * 1024),
        name="fine",
    )(count, slots, cubes, coarse_gate, query_input, key_input, value_input, coarse,
      recv.reshape(2, PLANE * NZ * SLOTS, TOK, HD))
    shape = (CUBES * TOK, HEADS * HD)
    return pl.pallas_call(
        project,
        out_shape=jax.ShapeDtypeStruct(shape, jnp.bfloat16),
        in_specs=[vmem_spec, any_spec],
        out_specs=vmem_spec,
        scratch_shapes=[
            pltpu.VMEM(shape, jnp.bfloat16),
            pltpu.VMEM((2 * HEADS * HD, HEADS * HD), jnp.bfloat16),
            pltpu.VMEM(shape, jnp.float32),
            dma, dma, dma,
        ],
        compiler_params=pltpu.CompilerParams(
            collective_id=1, has_side_effects=True, vmem_limit_bytes=60 * 1024 * 1024),
        name="project",
    )(attended, out_weight)


def solution(mesh):
    placed = (
        P("seq", "head"),
        P("seq", "head"),
        P("seq", "head"),
        P("seq", "head", None),
        P("head"),
        P(),
    )
    return jax.shard_map(
        body, mesh=mesh, in_specs=placed, out_specs=P("seq", "head"), check_vma=False
    )
```

time: 570 us -> 199 us (0.35)
  waiting for transfers between devices: 309 us -> 0 us
  Pallas kernels: 0 us -> 195 us
  local copies, waits for them, and re-layouts: 127 us -> 3.47 us
  matrix products: 74.5 us -> 0 us
  starting transfers between devices: 25 us -> 0 us
  other arithmetic: 17.3 us -> 0 us
  between operations: 13.4 us -> 0.03 us
    all_gather x2 -> x0, waiting for transfers between devices: 285 us -> none  [the longest x1 145 us: body(): lax.all_gather(pooled_v, 'seq', axis=0, tiled=True)]
    pallas_call x0 -> x3, Pallas kernels: none -> 195 us  [the longest x1 164 us: body(): pl.pallas_call(exchange, out_shape=(jax.ShapeDtypeStruct((2, PLANE * NZ,...]
    gather x7 -> x0, local copies, waits for them, and re-layouts: 85 us -> none  [the longest x4 63.4 us: fine_block(): remote = fetched_flat[block_pos]]
    dot_general x19 -> x0, matrix products: 74.5 us -> none  [the longest x4 36.9 us: fine_block(): jnp.einsum('bhqtk,bhtkd->bqhd', remote_w, remote_v, preferred_element_typ...]
    all_to_all x2 -> x0, starting transfers between devices: 24.9 us -> none  [the longest x1 16.5 us: body(): lax.all_to_all(slot_ids, 'seq', split_axis=0, concat_axis=0, tiled=True)]
    reduce_scatter x1 -> x0, waiting for transfers between devices: 18.4 us -> none  [body(): lax.psum_scatter(partial_terms, 'head', scatter_dimension=1, tiled=True)]
    while x12 -> x0, local copies, waits for them, and re-layouts: 13.7 us -> none
    reduce_sum x12 -> x0, other arithmetic: 10.9 us -> none  [the longest x8 10.2 us: fine_block(): totals = jnp.sum(remote_exp, axis=(3, 4)) + jnp.sum(own_exp, axis=3)]
  transfers between devices with their start and end apart: 5 -> 0, of which waited for: 4 -> 0; matrix products, arithmetic and copies ran while one was open for 6% -> 0% of each run, Pallas kernels for 0% -> 0%
where the time goes in v1:
time: 199 us; the launch traced here: 198 us
  Pallas kernels  195 us (98%)
  local copies, waits for them, and re-layouts  3.47 us (2%)
    pallas_call x1, Pallas kernels, body(): pl.pallas_call(exchange, out_shape=(jax.ShapeDtypeStruct((2, PLANE * NZ,...  164 us
    pallas_call x1, Pallas kernels, body(): pl.pallas_call(fine, out_shape=jax.ShapeDtypeStruct((CUBES * TOK, HEADS *...  23.2 us
    pallas_call x1, Pallas kernels, body(): pl.pallas_call(project, out_shape=jax.ShapeDtypeStruct(shape, jnp.bfloat1...  7.89 us

profile of v1, /device:TPU:1, one launch (start us, length us, event | category | flops | bytes accessed | tf_op | source)
XLA Modules:
  0.0 198.3 jit_solution(10669604126528705760)
XLA Ops:
  0.0 1.4 reshape.18.lists_ref
  1.4 163.8 %exchange.1 = (bf16[2,128,192,128]{3,2,1,0:T(8,128)(2,1)}, f32[48,128]{1,0:T(8,128)}, s32[6,128]{1,0:T(8,128)}, s32[6,256]{1,0:T(8,128)}, s32[6,256]{1,0:T(8,128)}) custom-call(bf16[8,64,768]{2,1,0:T(8,128)(2,1)} %bitcast.6, bf16[8,64,768]{2,1,0:T(8,128)(2,1)} %bitcast.7, bf16[8,64,768]{2,1,0:T(8,128)(2,1)} %bitcast.8, s32[6,256]{1,0:T(8,128)} %reshape.18.lists_ref), custom_call_target="tpu_custom_call" | custom-call | tf_op jit(solution)/shard_map/exchange/pallas_call | solution.py:463
  165.2 23.2 %fine.1.att_ref = bf16[512,768]{1,0:T(8,128)(2,1)} custom-call(s32[6,128]{1,0:T(8,128)} %get-tuple-element.10.count_ref, s32[6,256]{1,0:T(8,128)} %get-tuple-element.11.slot_ref, s32[6,256]{1,0:T(8,128)} %get-tuple-element.12.bits_ref, f32[6]{0:T(128)} %gate_ref.1, bf16[512,768]{1,0:T(8,128)(2,1)} %q_ref.1, bf16[512,768]{1,0:T(8,128)(2,1)} %k_ref.1, ...), custom_call_target="tpu_custom_call" | custom-call | tf_op jit(solution)/shard_map/fine/pallas_call | solution.py:496
  188.4 7.9 %project.1 = bf16[512,768]{1,0:T(8,128)(2,1)} custom-call(bf16[512,768]{1,0:T(8,128)(2,1)} %fine.1.att_ref, bf16[1536,1536]{1,0:T(8,128)(2,1)} %w_hbm.1), custom_call_target="tpu_custom_call" | custom-call | tf_op jit(solution)/shard_map/project/pallas_call | solution.py:511
  196.3 2.1 %copy.8 = bf16[512,768]{1,0:T(8,128)(2,1)} copy(bf16[512,768]{1,0:T(8,128)(2,1)} %project.1) | data formatting | bytes 1572864

commit v2 on v1

--- a/solution.py
+++ b/solution.py
@@ -16,12 +16,14 @@
 HD = 128
 TOP = 32
 UNITS = CUBES * HEADS
-MAXU = 224
-GROUP = 16
-RING = MAXU // GROUP + 1
+MAXU = 144
+GROUP = 8
+RING = MAXU // GROUP
 NEG = -1e30
 AHEAD = 4
-PACK = SLOTS * TOK
+EARLY = {0: 0, 1: 1, 2: 2, 4: 3, 5: 4}
+LATE = {3: 0, 6: 1, 7: 2}
+SAFE = PLANE * SLOTS
 SCALE = HD ** -0.5
 LOG2E = 1.4426950408889634
 NT = (((1,), (1,)), ((), ()))
@@ -35,12 +37,13 @@
     return jnp.where(mask, 1.0, 0.0).astype(jnp.bfloat16)
 
 
-def unit_slots(lists_ref, table_ref, bits_ref, rank_ref):
+def unit_slots(z, lists_ref, table_ref, bits_ref, rank_ref, pos_ref):
     entry_bit = 1 << (iota((CUBES, 256), 1) >> 5)
-    bits = []
+    bits, hots = [], []
     for h in range(HEADS):
         row = lists_ref[h:h + 1, :]
         owner_hot = flag((row >> 3) == iota((128, 256), 0))
+        hots.append(owner_hot)
         within_bit = jnp.where((row & 7) == iota((CUBES, 256), 0), entry_bit, 0)
         bits.append(lax.dot_general(within_bit.astype(jnp.float32).astype(jnp.bfloat16), owner_hot, NT,
                                     preferred_element_type=jnp.float32))
@@ -54,14 +57,28 @@
     table_ref[...] = jnp.zeros_like(table_ref)
     for s in range(SLOTS):
         table_ref[s:s + 1, :] = jnp.sum(jnp.where(need & (rank == s + 1), unit, 0), axis=0, keepdims=True)
-
-
-def head_lists(bits_ref, rank_ref, count_ref, slots_ref, cubes_ref):
+    pos_ref[...] = jnp.zeros_like(pos_ref)
+    for h in range(HEADS):
+        row = lists_ref[h:h + 1, :]
+        owner = row >> 3
+        spread = jnp.dot(rank[h * 8:h * 8 + 8].astype(jnp.bfloat16), hots[h], preferred_element_type=jnp.float32)
+        here = jnp.where((row & 7) == iota((CUBES, 256), 0), spread, 0.0)
+        order = jnp.sum(here, axis=0, keepdims=True).astype(jnp.int32) - 1
+        ahead = (((owner >> 2) & 7) - z) & 7
+        which = jnp.where(ahead == 0, 0, jnp.where(ahead >= 6, 8 - ahead, ahead + 2))
+        column = (owner >> 5) * NX + (owner & 3)
+        late = (ahead >= 3) & (ahead <= 5)
+        pos_ref[h:h + 1, :] = jnp.where(late, -1, (which * PLANE + column) * SLOTS + order)
+
+
+def head_lists(z, bits_ref, rank_ref, count_ref, slots_ref, cubes_ref):
     bits, rank = bits_ref[...], rank_ref[...]
     need = bits > 0
+    ahead = (((iota((UNITS, 128), 1) >> 2) & 7) - z) & 7
+    late = (ahead >= 3) & (ahead <= 5)
     mine, mine_bits = [], []
     for s in range(SLOTS):
-        hit = jnp.where(need & (rank == s + 1), 1.0, 0.0)
+        hit = jnp.where(need & (rank == s + 1) & late, 1.0, 0.0)
         seen = hit * bits
         mine.append([jnp.sum(hit[h * 8:h * 8 + 8], axis=0, keepdims=True) for h in range(HEADS)])
         mine_bits.append([jnp.sum(seen[h * 8:h * 8 + 8], axis=0, keepdims=True) for h in range(HEADS)])
@@ -69,7 +86,9 @@
     upper = flag(iota((wide, wide), 0) <= iota((wide, wide), 1))
     lane = iota((1, wide), 1)
     owner = lane & 127
-    place = ((owner >> 5) * NX + (owner & 3)) * NZ + ((owner >> 2) & 7)
+    ahead = (((owner >> 2) & 7) - z) & 7
+    index = jnp.where(ahead == 5, 0, jnp.where(ahead == 3, 1, 2))
+    place = ((owner >> 5) * NX + (owner & 3)) * len(LATE) + index
     place = jnp.broadcast_to(place.astype(jnp.float32), (8, wide))
     slot = jnp.broadcast_to((lane >> 7).astype(jnp.float32), (8, wide))
     sub = iota((8, wide), 0)
@@ -89,14 +108,14 @@
 
 
 def exchange(
-    q_hbm, k_hbm, v_hbm, lists_ref, recv, coarse_ref, count_ref, slots_ref, cubes_ref, *scratch
+    q_hbm, k_hbm, v_hbm, lists_ref, recv, coarse_ref, count_ref, slots_ref, cubes_ref, part_ref, stat_ref, *scratch
 ):
     q_own = scratch[0]
     kk = scratch[1:9]
     vv = scratch[9:17]
-    (send_buf, tbl_ref, bits_ref, rank_ref, tbl_all, tbl_sm, q_all, pool_k, pool_v, o_res, o_half, o_got, stats, stats_all,
+    (send_buf, early, tbl_ref, bits_ref, rank_ref, pos_ref, pos_sm, tbl_all, tbl_sm, q_all, pool_k, pool_v, o_res, o_half, o_got, stats, stats_all,
      load_sem, z_send, z_recv, t_send, t_recv, q_send, q_recv, u_send, u_recv,
-     o_send, o_recv, m_send, m_recv, sm_sem, loc_sem) = scratch[17:]
+     o_send, o_recv, m_send, m_recv, sm_sem, pos_sem, loc_sem) = scratch[17:]
     s = lax.axis_index("seq")
     x = lax.rem(s, NX)
     z = lax.rem(lax.div(s, NX), NZ)
@@ -133,7 +152,7 @@
     def _(j):
         pl.semaphore_signal(barrier, inc=1, device_id={"seq": peer(j)[1]}, device_id_type=pl.DeviceIdType.MESH)
 
-    unit_slots(lists_ref, tbl_ref, bits_ref, rank_ref)
+    unit_slots(z, lists_ref, tbl_ref, bits_ref, rank_ref, pos_ref)
     pl.semaphore_wait(barrier, PLANE + 1)
 
     @pl.loop(1, PLANE)
@@ -184,9 +203,12 @@
         pp, seq = peer(j)
         remote(tbl_ref, tbl_all.at[pp], t_send.at[j], t_recv.at[pp], seq).wait()
 
+    to_smem_pos = pltpu.make_async_copy(pos_ref, pos_sm, pos_sem)
+    to_smem_pos.start()
     to_smem = pltpu.make_async_copy(tbl_all, tbl_sm, sm_sem)
     to_smem.start()
     to_smem.wait()
+    to_smem_pos.wait()
 
     def owner_z(k):
         if k <= 3:
@@ -195,28 +217,70 @@
             return lax.rem(z + k - 3, NZ)
         return lax.rem(z + 4, NZ)
 
-    def pick(k, val, pp):
+    def unit_of(k, val, pp, sl):
         lane = (y * NZ + owner_z(k)) * NX + x
-        src = vv[k] if val else kk[k]
-        for sl in range(SLOTS):
-            send_buf[val, k, pp, pl.ds(sl * TOK, TOK), :] = src[jnp.clip(tbl_sm[pp, sl, lane], 0, UNITS - 1)]
+        return (vv[k] if val else kk[k])[jnp.clip(tbl_sm[pp, sl, lane], 0, UNITS - 1)]
+
+    def landing(k, val, p):
+        if k in EARLY:
+            return early.at[val, pl.ds((EARLY[k] * PLANE + p) * SLOTS, SLOTS)]
+        return recv.at[val, pl.ds((p * len(LATE) + LATE[k]) * SLOTS, SLOTS)]
 
     def own_copy(k, val):
-        return pltpu.make_async_copy(send_buf.at[val, k, me], recv.at[val, me * NZ + owner_z(k)], loc_sem.at[val, k])
+        return pltpu.make_async_copy(send_buf.at[val, k, me], landing(k, val, me), loc_sem.at[val, LATE[k]])
 
     def handle(k, val):
-        oz = owner_z(k)
-
         @pl.loop(1, PLANE)
         def _(j):
             pp, seq = peer(j)
-            pick(k, val, pp)
-            remote(send_buf.at[val, k, pp], recv.at[val, me * NZ + oz],
-                   u_send.at[val, k, j], u_recv.at[val, oz, me], seq).start()
-
-        if k > 0:
-            pick(k, val, me)
+            for sl in range(SLOTS):
+                send_buf[val, k, pp, sl] = unit_of(k, val, pp, sl)
+            remote(send_buf.at[val, k, pp], landing(k, val, me), u_send.at[val, k, j], u_recv.at[val, k, me], seq).start()
+
+        for sl in range(SLOTS):
+            if k in LATE:
+                send_buf[val, k, me, sl] = unit_of(k, val, me, sl)
+            elif k > 0:
+                early[val, (EARLY[k] * PLANE + me) * SLOTS + sl] = unit_of(k, val, me, sl)
+        if k in LATE:
             own_copy(k, val).start()
+
+    def arrived(k, val):
+        @pl.loop(1, PLANE)
+        def _(j):
+            pp, seq = peer(j)
+            remote(send_buf.at[val, k, pp], landing(k, val, pp), u_send.at[val, k, j], u_recv.at[val, k, pp], seq).wait_recv()
+
+    low_lanes = iota((1, 128), 1) < TOK
+
+    def attend(i):
+        h, c = lax.div(i, CUBES), lax.rem(i, CUBES)
+        q = q_own[i]
+        scores = [lax.dot_general(q, kk[0][i], NT, preferred_element_type=jnp.float32)]
+        spots = [pos_sm[h, c * TOP + t] for t in range(TOP)]
+        where = [jnp.clip(jnp.where(p < 0, SAFE, p), 0, len(EARLY) * PLANE * SLOTS - 1) for p in spots]
+        bias = [jnp.where(p < 0, NEG, 0.0) for p in spots]
+        for g in range(TOP // 4):
+            keys = jnp.concatenate([early[0, where[4 * g + t]] for t in range(4)], axis=0)
+            sc = lax.dot_general(q, keys, NT, preferred_element_type=jnp.float32)
+            hide = jnp.concatenate(
+                [jnp.where(low_lanes, bias[4 * g + t], bias[4 * g + t + 1]) for t in (0, 2)], axis=1)
+            scores.append(sc + hide)
+        top = functools.reduce(jnp.maximum, scores[1:])
+        top = jnp.maximum(jnp.max(top, axis=1, keepdims=True), jnp.max(scores[0], axis=1, keepdims=True))
+        es = [jnp.exp2((sc - top) * (SCALE * LOG2E)) for sc in scores]
+        tot = jnp.sum(es[0], axis=1, keepdims=True) + jnp.sum(sum(es[2:], es[1]), axis=1, keepdims=True)
+        acc = jnp.dot(es[0].astype(jnp.bfloat16), vv[0][i], preferred_element_type=jnp.float32)
+        for g in range(TOP // 4):
+            vals = jnp.concatenate([early[1, where[4 * g + t]] for t in range(4)], axis=0)
+            acc += jnp.dot(es[g + 1].astype(jnp.bfloat16), vals, preferred_element_type=jnp.float32)
+        part_ref[i] = acc
+        stat_ref[i] = jnp.where(low_lanes, top, tot)
+
+    def attend_range(lo, hi):
+        @pl.loop(lo, hi)
+        def _(i):
+            attend(i)
 
     def pool(k, val):
         src, dst = (vv[k], pool_v) if val else (kk[k], pool_k)
@@ -230,7 +294,7 @@
     handle(0, 1)
     pool(0, 0)
     pool(0, 1)
-    head_lists(bits_ref, rank_ref, count_ref, slots_ref, cubes_ref)
+    head_lists(z, bits_ref, rank_ref, count_ref, slots_ref, cubes_ref)
     for n in range(14):
         for way in (to_right, to_left):
             way[n].wait_recv()
@@ -243,6 +307,15 @@
                 if stage < 3:
                     handle(k, which)
                 pool(k, which)
+        if n == 10:
+            for k in EARLY:
+                arrived(k, 0)
+                arrived(k, 1)
+            attend_range(0, 8)
+        if n == 11:
+            attend_range(8, 22)
+        if n == 12:
+            attend_range(22, 30)
 
     @pl.loop(1, PLANE)
     def _(j):
@@ -276,6 +349,7 @@
 
     handle(7, 0)
     handle(7, 1)
+    attend_range(30, UNITS)
     o_got[me] = o_half[me]
     stats_all[me] = stats[me]
 
@@ -297,34 +371,31 @@
     for c in to_right + to_left:
         c.wait_send()
     for k in range(NZ):
-        oz = owner_z(k)
         for val in range(2):
-            if k > 0:
+            if k in LATE:
                 own_copy(k, val).wait()
+                arrived(k, val)
 
             @pl.loop(1, PLANE)
             def _(j):
                 pp, seq = peer(j)
-                remote(send_buf.at[val, k, pp], recv.at[val, pp * NZ + oz],
-                       u_send.at[val, k, j], u_recv.at[val, oz, pp], seq).wait()
-
-
-def fine(count_ref, slot_ref, bits_ref, gate_ref, q_ref, k_ref, v_ref, coarse_ref, recv_hbm, out_ref,
-         recv, s_buf, s_own, top, peak, tot, acc, sem):
+                remote(send_buf.at[val, k, pp], landing(k, val, me), u_send.at[val, k, j], u_recv.at[val, k, me], seq).wait_send()
+
+
+def fine(count_ref, slot_ref, bits_ref, gate_ref, q_ref, part_ref, stat_ref, coarse_ref, recv_hbm, out_ref,
+         recv, s_buf, top, peak, tot, acc, sem):
     c2 = SCALE * LOG2E
     pairs = GROUP // 2
     copies = [pltpu.make_async_copy(recv_hbm.at[i], recv.at[i], sem.at[i]) for i in range(2)]
     for c in copies:
         c.start()
-    same = (lax.broadcasted_iota(jnp.int32, (128, 128), 0) < TOK) == (
-        lax.broadcasted_iota(jnp.int32, (128, 128), 1) < TOK)
     lane = lax.broadcasted_iota(jnp.int32, (1, 128), 1)
 
     def columns(h):
         return pl.ds(pl.multiple_of(h * HD, HD), HD)
 
     def blocks(h):
-        return lax.div(count_ref[jnp.minimum(h, HEADS - 1), 0] + GROUP - 1, GROUP)
+        return jnp.maximum(lax.div(count_ref[jnp.minimum(h, HEADS - 1), 0] + GROUP - 1, GROUP), 1)
 
     def step(at):
         h, g = at
@@ -333,7 +404,7 @@
 
     def units(val, h, g):
         return jnp.concatenate(
-            [recv[val, slot_ref[h, jnp.minimum(g * GROUP + t, count_ref[h, 0] - 1)]] for t in range(GROUP)], axis=0)
+            [recv[val, slot_ref[h, jnp.clip(count_ref[h, 0] - 1, 0, g * GROUP + t)]] for t in range(GROUP)], axis=0)
 
     def score(i, at):
         h, g = at
@@ -359,12 +430,12 @@
         @pl.when(g == 0)
         def _():
             peak[...] = jnp.broadcast_to(jnp.max(top[h], axis=1, keepdims=True) * c2, (CUBES * TOK, HD))
-            for c in range(CUBES // 2):
-                rows = pl.ds(c * 128, 128)
-                e = jnp.exp2(s_own[h, rows, :] * c2 - peak[rows, :])
-                tot[rows, :] = e
-                acc[rows, :] = jnp.dot(
-                    e.astype(jnp.bfloat16), v_ref[rows, columns(h)], preferred_element_type=jnp.float32)
+            for c in range(CUBES):
+                rows = pl.ds(c * TOK, TOK)
+                state = stat_ref[h * CUBES + c]
+                shrink = jnp.exp2(state[:, 0:1] * c2 - peak[rows, :])
+                tot[rows, :] = shrink * (state[:, TOK:TOK + 1] * (1.0 / HD))
+                acc[rows, :] = shrink * part_ref[h * CUBES + c]
 
     def value(i, at):
         h, g = at
@@ -393,15 +464,10 @@
                 pooled = gate_ref[h] * coarse_ref[pl.ds(h * CUBES + c, 1), :]
                 out_ref[rows, columns(h)] = (acc[rows, :] / total + pooled).astype(jnp.bfloat16)
 
-    @pl.loop(0, HEADS)
-    def _(h):
-        for c in range(CUBES // 2):
-            rows = pl.ds(c * 128, 128)
-            sc = lax.dot_general(
-                q_ref[rows, columns(h)], k_ref[rows, columns(h)], NT, preferred_element_type=jnp.float32)
-            sc = jnp.where(same, sc, NEG)
-            s_own[h, rows, :] = sc
-            top[h, rows, :] = sc
+    @pl.loop(0, UNITS)
+    def _(i):
+        top[lax.div(i, CUBES), pl.ds(pl.multiple_of(lax.rem(i, CUBES) * TOK, TOK), TOK), :] = jnp.broadcast_to(
+            stat_ref[i][:, 0:1], (TOK, HD))
 
     longest, items = blocks(0), blocks(0)
     for h in range(1, HEADS):
@@ -460,22 +526,27 @@
     vmem_spec = pl.BlockSpec(memory_space=pltpu.VMEM)
     smem_spec = pl.BlockSpec(memory_space=pltpu.SMEM)
     dma = pltpu.SemaphoreType.DMA
-    recv, coarse, count, slots, cubes = pl.pallas_call(
+    recv, coarse, count, slots, cubes, part, stat = pl.pallas_call(
         exchange,
         out_shape=(
-            jax.ShapeDtypeStruct((2, PLANE * NZ, PACK, HD), jnp.bfloat16),
+            jax.ShapeDtypeStruct((2, PLANE * len(LATE) * SLOTS, TOK, HD), jnp.bfloat16),
             jax.ShapeDtypeStruct((UNITS, HD), jnp.float32),
             jax.ShapeDtypeStruct((HEADS, 128), jnp.int32),
             jax.ShapeDtypeStruct((HEADS, 256), jnp.int32),
             jax.ShapeDtypeStruct((HEADS, 256), jnp.int32),
+            jax.ShapeDtypeStruct((UNITS, TOK, HD), jnp.float32),
+            jax.ShapeDtypeStruct((UNITS, TOK, HD), jnp.float32),
         ),
         in_specs=[any_spec] * 3 + [vmem_spec],
-        out_specs=(any_spec,) + (vmem_spec,) * 4,
+        out_specs=(any_spec,) + (vmem_spec,) * 6,
         scratch_shapes=[pltpu.VMEM((UNITS, TOK, HD), jnp.bfloat16)] * 17 + [
-            pltpu.VMEM((2, NZ, PLANE, PACK, HD), jnp.bfloat16),
+            pltpu.VMEM((2, NZ, PLANE, SLOTS, TOK, HD), jnp.bfloat16),
+            pltpu.VMEM((2, len(EARLY) * PLANE * SLOTS, TOK, HD), jnp.bfloat16),
             pltpu.VMEM((8, 128), jnp.int32),
             pltpu.VMEM((UNITS, 128), jnp.float32),
             pltpu.VMEM((UNITS, 128), jnp.float32),
+            pltpu.VMEM((8, 256), jnp.int32),
+            pltpu.SMEM((8, 256), jnp.int32),
             pltpu.VMEM((PLANE, 8, 128), jnp.int32),
             pltpu.SMEM((PLANE, 8, 128), jnp.int32),
             pltpu.VMEM((PLANE, UNITS, HD), jnp.float32),
@@ -487,7 +558,7 @@
             pltpu.VMEM((PLANE, CUBES, HD), jnp.float32),
             pltpu.VMEM((PLANE, CUBES, HD), jnp.float32),
             dma((18,)), dma((28,)), dma((28,)), dma((PLANE,)), dma((PLANE,)), dma((PLANE,)), dma((PLANE,)),
-            dma((2, NZ, PLANE)), dma((2, NZ, PLANE)), dma((PLANE,)), dma((PLANE,)), dma((PLANE,)), dma((PLANE,)), dma, dma((2, NZ)),
+            dma((2, NZ, PLANE)), dma((2, NZ, PLANE)), dma((PLANE,)), dma((PLANE,)), dma((PLANE,)), dma((PLANE,)), dma, dma, dma((2, len(LATE))),
         ],
         compiler_params=pltpu.CompilerParams(
             collective_id=0, has_side_effects=True, vmem_limit_bytes=56 * 1024 * 1024),
@@ -499,14 +570,13 @@
         in_specs=[smem_spec] * 4 + [vmem_spec] * 4 + [any_spec],
         out_specs=vmem_spec,
         scratch_shapes=[
-            pltpu.VMEM((2, PLANE * NZ * SLOTS, TOK, HD), jnp.bfloat16),
+            pltpu.VMEM((2, PLANE * len(LATE) * SLOTS, TOK, HD), jnp.bfloat16),
             pltpu.VMEM((RING, GROUP // 2, CUBES * TOK, HD), jnp.float32),
-        ] + [pltpu.VMEM((HEADS, CUBES * TOK, HD), jnp.float32)] * 2 + [pltpu.VMEM((CUBES * TOK, HD), jnp.float32)] * 3
+        ] + [pltpu.VMEM((HEADS, CUBES * TOK, HD), jnp.float32)] + [pltpu.VMEM((CUBES * TOK, HD), jnp.float32)] * 3
         + [dma((2,))],
         compiler_params=pltpu.CompilerParams(vmem_limit_bytes=56 * 1024 * 1024),
         name="fine",
-    )(count, slots, cubes, coarse_gate, query_input, key_input, value_input, coarse,
-      recv.reshape(2, PLANE * NZ * SLOTS, TOK, HD))
+    )(count, slots, cubes, coarse_gate, query_input, part, stat, coarse, recv)
     shape = (CUBES * TOK, HEADS * HD)
     return pl.pallas_call(
         project,
@@ -520,7 +590,7 @@
             dma, dma, dma,
         ],
         compiler_params=pltpu.CompilerParams(
-            collective_id=1, has_side_effects=True, vmem_limit_bytes=60 * 1024 * 1024),
+            collective_id=1, has_side_effects=True, vmem_limit_bytes=48 * 1024 * 1024),
         name="project",
     )(attended, out_weight)
 

time: 199 us -> 193 us (0.970)
  Pallas kernels: 195 us -> 189 us
    pallas_call x1, Pallas kernels: 23.2 us -> 18.9 us  [body(): pl.pallas_call(fine, out_shape=jax.ShapeDtypeStruct((CUBES * TOK, HEADS *...]
where the time goes in v2:
time: 193 us; the launch traced here: 192 us
  Pallas kernels  189 us (98%)
  local copies, waits for them, and re-layouts  3.42 us (2%)
    pallas_call x1, Pallas kernels, body(): pl.pallas_call(exchange, out_shape=(jax.ShapeDtypeStruct((2, PLANE * len(...  164 us
    pallas_call x1, Pallas kernels, body(): pl.pallas_call(fine, out_shape=jax.ShapeDtypeStruct((CUBES * TOK, HEADS *...  18.9 us
    pallas_call x1, Pallas kernels, body(): pl.pallas_call(project, out_shape=jax.ShapeDtypeStruct(shape, jnp.bfloat1...  6.4 us

profile of v2, /device:TPU:1, one launch (start us, length us, event | category | flops | bytes accessed | tf_op | source)
XLA Modules:
  0.0 192.4 jit_solution(17152456796146177756)
XLA Ops:
  0.0 1.4 reshape.15.lists_ref
  1.4 163.7 %exchange.1 = (bf16[2,144,64,128]{3,2,1,0:T(8,128)(2,1)}, f32[48,128]{1,0:T(8,128)}, s32[6,128]{1,0:T(8,128)}, s32[6,256]{1,0:T(8,128)}, s32[6,256]{1,0:T(8,128)...) custom-call(bf16[8,64,768]{2,1,0:T(8,128)(2,1)} %bitcast.4, bf16[8,64,768]{2,1,0:T(8,128)(2,1)} %bitcast.5, ...), custom_call_target="tpu_custom_call" | custom-call | tf_op jit(solution)/shard_map/exchange/pallas_call | solution.py:529
  165.1 18.9 %fine.1.att_ref = bf16[512,768]{1,0:T(8,128)(2,1)} custom-call(s32[6,128]{1,0:T(8,128)} %get-tuple-element.12.count_ref, s32[6,256]{1,0:T(8,128)} %get-tuple-element.13.slot_ref, s32[6,256]{1,0:T(8,128)} %get-tuple-element.14.bits_ref, f32[6]{0:T(128)} %gate_ref.1, bf16[512,768]{1,0:T(8,128)(2,1)} %q_ref.1, f32[48,64,128]{2,1,0:T(8,128)} %get-tuple-element.15.part_ref, ...), custom_call_target="tpu_custom_call" | custom-call | tf_op jit(solution)/shard_map/fine/pallas_call | solution.py:567
  184.0 0.0 copy-start
  184.0 1.1 copy-done
  185.1 6.4 %project.1 = bf16[512,768]{1,0:T(8,128)(2,1)S(1)} custom-call(bf16[512,768]{1,0:T(8,128)(2,1)S(1)} %copy-done, bf16[1536,1536]{1,0:T(8,128)(2,1)} %w_hbm.1), custom_call_target="tpu_custom_call" | custom-call | tf_op jit(solution)/shard_map/project/pallas_call | solution.py:581
  191.5 0.9 copy.8
Async XLA Ops:
  184.0 1.1 copy-start

commit v3 on v2

--- a/solution.py
+++ b/solution.py
@@ -37,14 +37,23 @@
     return jnp.where(mask, 1.0, 0.0).astype(jnp.bfloat16)
 
 
-def unit_slots(z, lists_ref, table_ref, bits_ref, rank_ref, pos_ref):
+def list_rows(lists_ref, owner_ref, within_ref):
+    spread = flag((iota((TOP, 256), 1) & (TOP - 1)) == iota((TOP, 256), 0))
+    mine = (iota((CUBES, 256), 1) >> 5) == iota((CUBES, 256), 0)
+    for h in range(HEADS):
+        cubes = lists_ref[:, h, :]
+        for part, ref in ((cubes >> 3, owner_ref), (cubes & 7, within_ref)):
+            wide = jnp.dot(part.astype(jnp.float32).astype(jnp.bfloat16), spread, preferred_element_type=jnp.float32)
+            ref[h:h + 1, :] = jnp.sum(jnp.where(mine, wide, 0.0), axis=0, keepdims=True).astype(jnp.int32)
+
+
+def unit_slots(z, owner_ref, within_ref, table_ref, bits_ref, rank_ref, pos_ref):
     entry_bit = 1 << (iota((CUBES, 256), 1) >> 5)
     bits, hots = [], []
     for h in range(HEADS):
-        row = lists_ref[h:h + 1, :]
-        owner_hot = flag((row >> 3) == iota((128, 256), 0))
+        owner_hot = flag(owner_ref[h:h + 1, :] == iota((128, 256), 0))
         hots.append(owner_hot)
-        within_bit = jnp.where((row & 7) == iota((CUBES, 256), 0), entry_bit, 0)
+        within_bit = jnp.where(within_ref[h:h + 1, :] == iota((CUBES, 256), 0), entry_bit, 0)
         bits.append(lax.dot_general(within_bit.astype(jnp.float32).astype(jnp.bfloat16), owner_hot, NT,
                                     preferred_element_type=jnp.float32))
     bits = jnp.concatenate(bits, axis=0)
@@ -59,10 +68,9 @@
         table_ref[s:s + 1, :] = jnp.sum(jnp.where(need & (rank == s + 1), unit, 0), axis=0, keepdims=True)
     pos_ref[...] = jnp.zeros_like(pos_ref)
     for h in range(HEADS):
-        row = lists_ref[h:h + 1, :]
-        owner = row >> 3
+        owner = owner_ref[h:h + 1, :]
         spread = jnp.dot(rank[h * 8:h * 8 + 8].astype(jnp.bfloat16), hots[h], preferred_element_type=jnp.float32)
-        here = jnp.where((row & 7) == iota((CUBES, 256), 0), spread, 0.0)
+        here = jnp.where(within_ref[h:h + 1, :] == iota((CUBES, 256), 0), spread, 0.0)
         order = jnp.sum(here, axis=0, keepdims=True).astype(jnp.int32) - 1
         ahead = (((owner >> 2) & 7) - z) & 7
         which = jnp.where(ahead == 0, 0, jnp.where(ahead >= 6, 8 - ahead, ahead + 2))
@@ -113,7 +121,7 @@
     q_own = scratch[0]
     kk = scratch[1:9]
     vv = scratch[9:17]
-    (send_buf, early, tbl_ref, bits_ref, rank_ref, pos_ref, pos_sm, tbl_all, tbl_sm, q_all, pool_k, pool_v, o_res, o_half, o_got, stats, stats_all,
+    (send_buf, early, owner_rows, within_rows, tbl_ref, bits_ref, rank_ref, pos_ref, pos_sm, tbl_all, tbl_sm, q_all, pool_k, pool_v, o_res, o_half, o_got, stats, stats_all,
      load_sem, z_send, z_recv, t_send, t_recv, q_send, q_recv, u_send, u_recv,
      o_send, o_recv, m_send, m_recv, sm_sem, pos_sem, loc_sem) = scratch[17:]
     s = lax.axis_index("seq")
@@ -152,7 +160,8 @@
     def _(j):
         pl.semaphore_signal(barrier, inc=1, device_id={"seq": peer(j)[1]}, device_id_type=pl.DeviceIdType.MESH)
 
-    unit_slots(z, lists_ref, tbl_ref, bits_ref, rank_ref, pos_ref)
+    list_rows(lists_ref, owner_rows, within_rows)
+    unit_slots(z, owner_rows, within_rows, tbl_ref, bits_ref, rank_ref, pos_ref)
     pl.semaphore_wait(barrier, PLANE + 1)
 
     @pl.loop(1, PLANE)
@@ -382,11 +391,12 @@
                 remote(send_buf.at[val, k, pp], landing(k, val, me), u_send.at[val, k, j], u_recv.at[val, k, me], seq).wait_send()
 
 
-def fine(count_ref, slot_ref, bits_ref, gate_ref, q_ref, part_ref, stat_ref, coarse_ref, recv_hbm, out_ref,
-         recv, s_buf, top, peak, tot, acc, sem):
+def fine(count_ref, slot_ref, bits_ref, gate_ref, q_ref, stat_ref, coarse_ref, part_hbm, recv_hbm, out_ref,
+         recv, part_ref, s_buf, top, peak, tot, acc, sem):
     c2 = SCALE * LOG2E
     pairs = GROUP // 2
     copies = [pltpu.make_async_copy(recv_hbm.at[i], recv.at[i], sem.at[i]) for i in range(2)]
+    copies.append(pltpu.make_async_copy(part_hbm, part_ref, sem.at[2]))
     for c in copies:
         c.start()
     lane = lax.broadcasted_iota(jnp.int32, (1, 128), 1)
@@ -434,7 +444,7 @@
                 rows = pl.ds(c * TOK, TOK)
                 state = stat_ref[h * CUBES + c]
                 shrink = jnp.exp2(state[:, 0:1] * c2 - peak[rows, :])
-                tot[rows, :] = shrink * (state[:, TOK:TOK + 1] * (1.0 / HD))
+                tot[rows, :] = shrink * jnp.where(lane < TOK, 0.0, state * (1.0 / TOK))
                 acc[rows, :] = shrink * part_ref[h * CUBES + c]
 
     def value(i, at):
@@ -466,8 +476,8 @@
 
     @pl.loop(0, UNITS)
     def _(i):
-        top[lax.div(i, CUBES), pl.ds(pl.multiple_of(lax.rem(i, CUBES) * TOK, TOK), TOK), :] = jnp.broadcast_to(
-            stat_ref[i][:, 0:1], (TOK, HD))
+        rows = pl.ds(pl.multiple_of(lax.rem(i, CUBES) * TOK, TOK), TOK)
+        top[lax.div(i, CUBES), rows, :] = jnp.where(lane < TOK, stat_ref[i], NEG)
 
     longest, items = blocks(0), blocks(0)
     for h in range(1, HEADS):
@@ -495,33 +505,36 @@
     zero = jnp.int32(0)
     ahead = lax.fori_loop(0, longest, only_score, (zero, zero))
     copies[1].wait()
+    copies[2].wait()
     ahead, at = lax.fori_loop(longest, items, both, (ahead, (zero, zero)))
     lax.fori_loop(items, items + longest, only_value, at)
 
 
-def project(att_ref, w_hbm, out_ref, other, w_buf, total, send_sem, recv_sem, w_sem):
+def project(att_hbm, w_hbm, out_ref, own, other, w_buf, total, send_sem, recv_sem, w_sem, own_sem):
     head = lax.axis_index("head")
     width = HEADS * HD
     weights = pltpu.make_async_copy(w_hbm.at[:, pl.ds(pl.multiple_of(head * width, width), width)], w_buf, w_sem)
+    fetch = pltpu.make_async_copy(att_hbm, own, own_sem)
+    fetch.start()
     weights.start()
     barrier = pltpu.get_barrier_semaphore()
     pl.semaphore_signal(barrier, inc=1, device_id={"head": 1 - head}, device_id_type=pl.DeviceIdType.MESH)
     pl.semaphore_wait(barrier, 1)
     swap = pltpu.make_async_remote_copy(
-        src_ref=att_ref, dst_ref=other, send_sem=send_sem, recv_sem=recv_sem,
+        src_ref=att_hbm, dst_ref=other, send_sem=send_sem, recv_sem=recv_sem,
         device_id={"head": 1 - head}, device_id_type=pl.DeviceIdType.MESH)
     swap.start()
+    fetch.wait()
     weights.wait()
     mine = pl.ds(pl.multiple_of(head * width, width), width)
     theirs = pl.ds(pl.multiple_of((1 - head) * width, width), width)
-    total[...] = jnp.dot(att_ref[...], w_buf[mine, :], preferred_element_type=jnp.float32)
+    total[...] = jnp.dot(own[...], w_buf[mine, :], preferred_element_type=jnp.float32)
     swap.wait()
     out_ref[...] = (
         total[...] + jnp.dot(other[...], w_buf[theirs, :], preferred_element_type=jnp.float32)).astype(jnp.bfloat16)
 
 
 def body(query_input, key_input, value_input, cube_lists, coarse_gate, out_weight):
-    lists = jnp.transpose(cube_lists, (1, 0, 2)).reshape(HEADS, CUBES * TOP)
     any_spec = pl.BlockSpec(memory_space=pl.ANY)
     vmem_spec = pl.BlockSpec(memory_space=pltpu.VMEM)
     smem_spec = pl.BlockSpec(memory_space=pltpu.SMEM)
@@ -542,6 +555,8 @@
         scratch_shapes=[pltpu.VMEM((UNITS, TOK, HD), jnp.bfloat16)] * 17 + [
             pltpu.VMEM((2, NZ, PLANE, SLOTS, TOK, HD), jnp.bfloat16),
             pltpu.VMEM((2, len(EARLY) * PLANE * SLOTS, TOK, HD), jnp.bfloat16),
+            pltpu.VMEM((8, 256), jnp.int32),
+            pltpu.VMEM((8, 256), jnp.int32),
             pltpu.VMEM((8, 128), jnp.int32),
             pltpu.VMEM((UNITS, 128), jnp.float32),
             pltpu.VMEM((UNITS, 128), jnp.float32),
@@ -563,31 +578,33 @@
         compiler_params=pltpu.CompilerParams(
             collective_id=0, has_side_effects=True, vmem_limit_bytes=56 * 1024 * 1024),
         name="exchange",
-    )(*[t.reshape(CUBES, TOK, HEADS * HD) for t in (query_input, key_input, value_input)], lists)
+    )(*[t.reshape(CUBES, TOK, HEADS * HD) for t in (query_input, key_input, value_input)], cube_lists)
     attended = pl.pallas_call(
         fine,
         out_shape=jax.ShapeDtypeStruct((CUBES * TOK, HEADS * HD), jnp.bfloat16),
-        in_specs=[smem_spec] * 4 + [vmem_spec] * 4 + [any_spec],
+        in_specs=[smem_spec] * 4 + [vmem_spec] * 3 + [any_spec] * 2,
         out_specs=vmem_spec,
         scratch_shapes=[
             pltpu.VMEM((2, PLANE * len(LATE) * SLOTS, TOK, HD), jnp.bfloat16),
+            pltpu.VMEM((UNITS, TOK, HD), jnp.float32),
             pltpu.VMEM((RING, GROUP // 2, CUBES * TOK, HD), jnp.float32),
         ] + [pltpu.VMEM((HEADS, CUBES * TOK, HD), jnp.float32)] + [pltpu.VMEM((CUBES * TOK, HD), jnp.float32)] * 3
-        + [dma((2,))],
+        + [dma((3,))],
         compiler_params=pltpu.CompilerParams(vmem_limit_bytes=56 * 1024 * 1024),
         name="fine",
-    )(count, slots, cubes, coarse_gate, query_input, part, stat, coarse, recv)
+    )(count, slots, cubes, coarse_gate, query_input, stat, coarse, part, recv)
     shape = (CUBES * TOK, HEADS * HD)
     return pl.pallas_call(
         project,
         out_shape=jax.ShapeDtypeStruct(shape, jnp.bfloat16),
-        in_specs=[vmem_spec, any_spec],
+        in_specs=[pl.BlockSpec(memory_space=pltpu.HBM)] * 2,
         out_specs=vmem_spec,
         scratch_shapes=[
             pltpu.VMEM(shape, jnp.bfloat16),
+            pltpu.VMEM(shape, jnp.bfloat16),
             pltpu.VMEM((2 * HEADS * HD, HEADS * HD), jnp.bfloat16),
             pltpu.VMEM(shape, jnp.float32),
-            dma, dma, dma,
+            dma, dma, dma, dma,
         ],
         compiler_params=pltpu.CompilerParams(
             collective_id=1, has_side_effects=True, vmem_limit_bytes=48 * 1024 * 1024),

time: 193 us -> 191 us (0.990)
  Pallas kernels: 189 us -> 187 us
    pallas_call x1, Pallas kernels: 18.9 us -> 15.1 us  [body(): pl.pallas_call(fine, out_shape=jax.ShapeDtypeStruct((CUBES * TOK, HEADS *...]
where the time goes in v3:
time: 191 us; the launch traced here: 190 us
  Pallas kernels  187 us (98%)
  local copies, waits for them, and re-layouts  3.37 us (2%)
    pallas_call x1, Pallas kernels, body(): pl.pallas_call(exchange, out_shape=(jax.ShapeDtypeStruct((2, PLANE * len(...  164 us
    pallas_call x1, Pallas kernels, body(): pl.pallas_call(fine, out_shape=jax.ShapeDtypeStruct((CUBES * TOK, HEADS *...  15.1 us
    pallas_call x1, Pallas kernels, body(): pl.pallas_call(project, out_shape=jax.ShapeDtypeStruct(shape, jnp.bfloat1...  7.97 us

profile of v3, /device:TPU:1, one launch (start us, length us, event | category | flops | bytes accessed | tf_op | source)
XLA Modules:
  0.0 190.2 jit_solution(8004617278937973582)
XLA Ops:
  0.0 1.4 copy.7.lists_ref
  1.4 163.8 %exchange.1 = (bf16[2,144,64,128]{3,2,1,0:T(8,128)(2,1)}, f32[48,128]{1,0:T(8,128)}, s32[6,128]{1,0:T(8,128)}, s32[6,256]{1,0:T(8,128)}, s32[6,256]{1,0:T(8,128)...) custom-call(bf16[8,64,768]{2,1,0:T(8,128)(2,1)} %bitcast.3, bf16[8,64,768]{2,1,0:T(8,128)(2,1)} %bitcast.4, ...), custom_call_target="tpu_custom_call" | custom-call | tf_op jit(solution)/shard_map/exchange/pallas_call | solution.py:542
  165.1 15.1 %fine.1.att_hbm = bf16[512,768]{1,0:T(8,128)(2,1)} custom-call(s32[6,128]{1,0:T(8,128)} %get-tuple-element.12.count_ref, s32[6,256]{1,0:T(8,128)} %get-tuple-element.13.slot_ref, s32[6,256]{1,0:T(8,128)} %get-tuple-element.14.bits_ref, f32[6]{0:T(128)} %gate_ref.1, bf16[512,768]{1,0:T(8,128)(2,1)} %q_ref.1, f32[48,64,128]{2,1,0:T(8,128)} %get-tuple-element.15.stat_ref, ...), custom_call_target="tpu_custom_call" | custom-call | tf_op jit(solution)/shard_map/fine/pallas_call | solution.py:582
  180.2 0.0 copy-start
  180.2 1.1 copy-done
  181.3 8.0 %project.1 = bf16[512,768]{1,0:T(8,128)(2,1)S(1)} custom-call(bf16[512,768]{1,0:T(8,128)(2,1)S(1)} %copy-done, bf16[1536,1536]{1,0:T(8,128)(2,1)} %w_hbm.1), custom_call_target="tpu_custom_call" | custom-call | tf_op jit(solution)/shard_map/project/pallas_call | solution.py:597
  189.3 0.9 copy.9
Async XLA Ops:
  180.2 1.1 copy-start

commit v4 on v3

--- a/solution.py
+++ b/solution.py
@@ -41,7 +41,7 @@
     spread = flag((iota((TOP, 256), 1) & (TOP - 1)) == iota((TOP, 256), 0))
     mine = (iota((CUBES, 256), 1) >> 5) == iota((CUBES, 256), 0)
     for h in range(HEADS):
-        cubes = lists_ref[:, h, :]
+        cubes = lists_ref[h]
         for part, ref in ((cubes >> 3, owner_ref), (cubes & 7, within_ref)):
             wide = jnp.dot(part.astype(jnp.float32).astype(jnp.bfloat16), spread, preferred_element_type=jnp.float32)
             ref[h:h + 1, :] = jnp.sum(jnp.where(mine, wide, 0.0), axis=0, keepdims=True).astype(jnp.int32)
@@ -576,9 +576,10 @@
             dma((2, NZ, PLANE)), dma((2, NZ, PLANE)), dma((PLANE,)), dma((PLANE,)), dma((PLANE,)), dma((PLANE,)), dma, dma, dma((2, len(LATE))),
         ],
         compiler_params=pltpu.CompilerParams(
-            collective_id=0, has_side_effects=True, vmem_limit_bytes=56 * 1024 * 1024),
+            collective_id=0, has_side_effects=True, vmem_limit_bytes=44 * 1024 * 1024),
         name="exchange",
-    )(*[t.reshape(CUBES, TOK, HEADS * HD) for t in (query_input, key_input, value_input)], cube_lists)
+    )(*[t.reshape(CUBES, TOK, HEADS * HD) for t in (query_input, key_input, value_input)],
+      jnp.transpose(cube_lists, (1, 0, 2)))
     attended = pl.pallas_call(
         fine,
         out_shape=jax.ShapeDtypeStruct((CUBES * TOK, HEADS * HD), jnp.bfloat16),
@@ -590,7 +591,7 @@
             pltpu.VMEM((RING, GROUP // 2, CUBES * TOK, HD), jnp.float32),
         ] + [pltpu.VMEM((HEADS, CUBES * TOK, HD), jnp.float32)] + [pltpu.VMEM((CUBES * TOK, HD), jnp.float32)] * 3
         + [dma((3,))],
-        compiler_params=pltpu.CompilerParams(vmem_limit_bytes=56 * 1024 * 1024),
+        compiler_params=pltpu.CompilerParams(vmem_limit_bytes=40 * 1024 * 1024),
         name="fine",
     )(count, slots, cubes, coarse_gate, query_input, stat, coarse, part, recv)
     shape = (CUBES * TOK, HEADS * HD)

time: 191 us -> 186 us (0.974)
  Pallas kernels: 187 us -> 181 us
  local copies, waits for them, and re-layouts: 3.37 us -> 5.67 us
    pallas_call x1, Pallas kernels: 15.1 us -> 12.1 us  [body(): pl.pallas_call(fine, out_shape=jax.ShapeDtypeStruct((CUBES * TOK, HEADS *...]
    unnamed x4 -> x11, local copies, waits for them, and re-layouts: 3.37 us -> 5.67 us
    pallas_call x1, Pallas kernels: 164 us -> 162 us  [body(): pl.pallas_call(exchange, out_shape=(jax.ShapeDtypeStruct((2, PLANE * len(...]
where the time goes in v4:
time: 186 us; the launch traced here: 187 us
  Pallas kernels  181 us (97%)
  local copies, waits for them, and re-layouts  5.67 us (3%)
    pallas_call x1, Pallas kernels, body(): pl.pallas_call(exchange, out_shape=(jax.ShapeDtypeStruct((2, PLANE * len(...  162 us
    pallas_call x1, Pallas kernels, body(): pl.pallas_call(fine, out_shape=jax.ShapeDtypeStruct((CUBES * TOK, HEADS *...  12.1 us
    pallas_call x1, Pallas kernels, body(): pl.pallas_call(project, out_shape=jax.ShapeDtypeStruct(shape, jnp.bfloat1...  7.33 us
    unnamed x11, local copies, waits for them, and re-layouts  5.67 us

profile of v4, /device:TPU:1, one launch (start us, length us, event | category | flops | bytes accessed | tf_op | source)
XLA Modules:
  0.0 186.8 jit_solution(4518822390157397060)
XLA Ops:
  0.0 0.0 copy-start
  0.0 1.1 copy-done
  1.1 0.0 copy-start.1
  1.1 1.1 copy-done.1
  2.3 0.0 copy-start.2
  2.3 1.1 copy-done.2
  3.4 0.0 copy-start.3
  3.4 0.7 copy-done.3
  4.1 161.7 %exchange.1 = (bf16[2,144,64,128]{3,2,1,0:T(8,128)(2,1)S(1)}, f32[48,128]{1,0:T(8,128)S(1)}, s32[6,128]{1,0:T(8,128)S(1)}, s32[6,256]{1,0:T(8,128)S(1)}, s32[6,2...) custom-call(bf16[8,64,768]{2,1,0:T(8,128)(2,1)S(1)} %bitcast.4, ...), custom_call_target="tpu_custom_call" | custom-call | tf_op jit(solution)/shard_map/exchange/pallas_call | solution.py:542
  165.8 0.0 copy-start.4
  165.8 0.6 copy-done.4
  166.5 12.1 %fine.1.att_hbm = bf16[512,768]{1,0:T(8,128)(2,1)S(1)} custom-call(s32[6,128]{1,0:T(8,128)S(1)} %get-tuple-element.12.count_ref, s32[6,256]{1,0:T(8,128)S(1)} %get-tuple-element.13.slot_ref, s32[6,256]{1,0:T(8,128)S(1)} %get-tuple-element.14.bits_ref, f32[6]{0:T(128)S(1)} %copy-done.4, bf16[512,768]{1,0:T(8,128)(2,1)S(1)} %copy-done, ...), custom_call_target="tpu_custom_call" | custom-call | tf_op jit(solution)/shard_map/fine/pallas_call | solution.py:583
  178.5 7.3 %project.1 = bf16[512,768]{1,0:T(8,128)(2,1)S(1)} custom-call(bf16[512,768]{1,0:T(8,128)(2,1)S(1)} %fine.1.att_hbm, bf16[1536,1536]{1,0:T(8,128)(2,1)} %w_hbm.1), custom_call_target="tpu_custom_call" | custom-call | tf_op jit(solution)/shard_map/project/pallas_call | solution.py:598
  185.9 0.9 copy.8
Async XLA Ops:
  0.0 1.1 copy-start
  1.1 1.1 copy-start.1
  2.3 1.1 copy-start.2
  3.4 0.7 copy-start.3
  165.8 0.7 copy-start.4

commit v5 on v4

--- a/solution.py
+++ b/solution.py
@@ -17,7 +17,7 @@
 TOP = 32
 UNITS = CUBES * HEADS
 MAXU = 144
-GROUP = 8
+GROUP = 4
 RING = MAXU // GROUP
 NEG = -1e30
 AHEAD = 4

time: 186 us -> 189 us (1.016); the launches traced: 187 us -> 188 us
  no operation moved by 1% of the time
where the time goes in v5:
time: 189 us; the launch traced here: 188 us
  Pallas kernels  182 us (96%)
  local copies, waits for them, and re-layouts  5.67 us (3%)
    pallas_call x1, Pallas kernels, body(): pl.pallas_call(exchange, out_shape=(jax.ShapeDtypeStruct((2, PLANE * len(...  162 us
    pallas_call x1, Pallas kernels, body(): pl.pallas_call(fine, out_shape=jax.ShapeDtypeStruct((CUBES * TOK, HEADS *...  12.7 us
    pallas_call x1, Pallas kernels, body(): pl.pallas_call(project, out_shape=jax.ShapeDtypeStruct(shape, jnp.bfloat1...  7.7 us
    unnamed x11, local copies, waits for them, and re-layouts  5.67 us

profile of v5, /device:TPU:1, one launch (start us, length us, event | category | flops | bytes accessed | tf_op | source)
XLA Modules:
  0.0 187.8 jit_solution(3949044887820491382)
XLA Ops:
  0.0 0.0 copy-start
  0.0 1.1 copy-done
  1.1 0.0 copy-start.1
  1.1 1.1 copy-done.1
  2.3 0.0 copy-start.2
  2.3 1.1 copy-done.2
  3.4 0.0 copy-start.3
  3.4 0.7 copy-done.3
  4.1 161.7 %exchange.1 = (bf16[2,144,64,128]{3,2,1,0:T(8,128)(2,1)S(1)}, f32[48,128]{1,0:T(8,128)S(1)}, s32[6,128]{1,0:T(8,128)S(1)}, s32[6,256]{1,0:T(8,128)S(1)}, s32[6,2...) custom-call(bf16[8,64,768]{2,1,0:T(8,128)(2,1)S(1)} %bitcast.4, ...), custom_call_target="tpu_custom_call" | custom-call | tf_op jit(solution)/shard_map/exchange/pallas_call | solution.py:542
  165.8 0.0 copy-start.4
  165.8 0.6 copy-done.4
  166.5 12.7 %fine.1.att_hbm = bf16[512,768]{1,0:T(8,128)(2,1)S(1)} custom-call(s32[6,128]{1,0:T(8,128)S(1)} %get-tuple-element.12.count_ref, s32[6,256]{1,0:T(8,128)S(1)} %get-tuple-element.13.slot_ref, s32[6,256]{1,0:T(8,128)S(1)} %get-tuple-element.14.bits_ref, f32[6]{0:T(128)S(1)} %copy-done.4, bf16[512,768]{1,0:T(8,128)(2,1)S(1)} %copy-done, ...), custom_call_target="tpu_custom_call" | custom-call | tf_op jit(solution)/shard_map/fine/pallas_call | solution.py:583
  179.2 7.7 %project.1 = bf16[512,768]{1,0:T(8,128)(2,1)S(1)} custom-call(bf16[512,768]{1,0:T(8,128)(2,1)S(1)} %fine.1.att_hbm, bf16[1536,1536]{1,0:T(8,128)(2,1)} %w_hbm.1), custom_call_target="tpu_custom_call" | custom-call | tf_op jit(solution)/shard_map/project/pallas_call | solution.py:598
  186.9 0.9 copy.8
Async XLA Ops:
  0.0 1.1 copy-start
  1.1 1.1 copy-start.1
  2.3 1.1 copy-start.2
  3.4 0.7 copy-start.3
  165.8 0.7 copy-start.4
